TPU v7x, 512 devices: a whole 4x4x16 slice. The times are simulated.
512 devices in a mesh: lon: 64 (over x, y, z_hi, core), lat: 8 (over z_lo).
Axes of the slice: x: 4, y: 4, z: 16 (z_hi: 2, z_lo: 8; z = z_hi * 8 + z_lo), core: 2. Of those that a mesh axis runs over, the one named last changes fastest.
Arguments:
- sketch: float32 [64, 1024, 2048], P(None, 'lon', 'lat'), may hold values from -6 to 6
- probe_bits: int32 [2, 1024, 2048], P(None, 'lon', 'lat'), may hold values from 0 to 65535
- ocean: int32 [1024, 2048], P('lon', 'lat'), may hold values 0 or 1
- east_cond: float32 [1024, 2048], P('lon', 'lat'), may hold values from 0.2 to 2
- north_cond: float32 [1024, 2048], P('lon', 'lat'), may hold values from 0.1 to 1
- kappa_sq: float32 [1024, 2048], P('lon', 'lat'), may hold values from 0.05 to 0.5
- inv_area: float32 [1024, 2048], P('lon', 'lat'), may hold values from 0.05 to 0.2
Outputs:
- image_out: float32 [64, 1024, 2048], P(None, 'lon', 'lat')
- gram_out: float32 [96, 96], replicated
Inputs may be any that keep to these rules, and one draw needn't show every extreme that they name: `probe_bits`: each word holds 16 independent sign bits, bit b of word w giving probe column 16 w + b.
All inputs are finite; a program needn't handle non-finite values. No bound on the sum of `ocean` on one device may be relied on, other than what follows from the above.
Results may differ from a plain program's by a relative error of at most 0.00015.
Values sent between devices are 32-bit elements; how exact they have to be, the bound alone decides.
A program may use at most 64 MiB of HBM per device.

v0:
```python
import jax
import jax.numpy as jnp
from jax import lax
from jax.sharding import PartitionSpec as P


def padded_2(cells, sides, width, closed):
    for axis, dim in sides:
        count = lax.axis_size(axis)
        ends = count if closed else count - 1
        head = lax.slice_in_dim(cells, 0, width, axis=dim)
        tail = lax.slice_in_dim(cells, cells.shape[dim] - width, cells.shape[dim], axis=dim)
        cells = jnp.concatenate(
            [
                lax.ppermute(tail, axis, [(i, (i + 1) % count) for i in range(ends)]),
                cells,
                lax.ppermute(head, axis, [((i + 1) % count, i) for i in range(ends)]),
            ],
            axis=dim,
        )
    return cells


def sign_columns(probe_bits):
    shifts = jnp.arange(16, dtype=jnp.int32)
    picked = jnp.right_shift(probe_bits[:, None], shifts[None, :, None, None])
    flipped = jnp.bitwise_and(picked, 1)
    return (1 - 2 * flipped).astype(jnp.float32).reshape((-1,) + probe_bits.shape[1:])


def operate(padded, weights):
    middle = padded[:, 1:-1, 1:-1]
    return weights[0] * (
        weights[1] * middle
        - weights[2] * padded[:, 2:, 1:-1]
        - weights[3] * padded[:, :-2, 1:-1]
        - weights[4] * padded[:, 1:-1, 2:]
        - weights[5] * padded[:, 1:-1, :-2]
    )


def extend(field_in, thickness):
    wider = padded_2(field_in, (("lon", 1),), thickness, True)
    return padded_2(wider, (("lat", 2),), thickness, False)


def pair_gram(left, right):
    left_flat = left.reshape(left.shape[0], -1)
    right_flat = right.reshape(right.shape[0], -1)
    return jnp.einsum("ac,bc->ab", left_flat, right_flat, precision=lax.Precision.HIGHEST)


def local(sketch, probe_bits, ocean, east_cond, north_cond, kappa_sq, inv_area):
    lon_count, lat_count = ocean.shape
    sea_mask = ocean.astype(jnp.float32)
    stacked = jnp.stack([sea_mask, east_cond, north_cond, kappa_sq, inv_area])
    widened = padded_2(stacked, (("lon", 1),), 2, True)
    widened = padded_2(widened, (("lat", 2),), 2, False)
    sea_wide = widened[0]
    east_wide = widened[1]
    north_wide = widened[2]
    kappa_wide = widened[3]
    area_wide = widened[4]
    east_edges = east_wide[:-1] * sea_wide[:-1] * sea_wide[1:]
    north_edges = north_wide[:, :-1] * sea_wide[:, :-1] * sea_wide[:, 1:]

    def region(margin):
        offset = 2 - margin
        span_lon = lon_count + 2 * margin
        span_lat = lat_count + 2 * margin

        def window(array, shift_lon, shift_lat):
            return array[
                offset + shift_lon : offset + shift_lon + span_lon,
                offset + shift_lat : offset + shift_lat + span_lat,
            ]

        east_weight = window(east_edges, 0, 0)
        west_weight = window(east_edges, -1, 0)
        north_weight = window(north_edges, 0, 0)
        south_weight = window(north_edges, 0, -1)
        center_term = (
            window(kappa_wide, 0, 0) + east_weight + west_weight + north_weight + south_weight
        )
        return (
            window(sea_wide, 0, 0),
            center_term,
            east_weight,
            west_weight,
            north_weight,
            south_weight,
            window(area_wide, 0, 0),
        )

    interior = region(0)
    sketch_masked = sketch * sea_mask
    columns = jnp.concatenate([sketch_masked, sign_columns(probe_bits) * sea_mask], axis=0)
    sketch_count = sketch.shape[0]
    thickness = 2
    columns_wide = extend(columns, thickness)
    exterior = region(1)
    first_wide = operate(columns_wide, exterior)
    second = operate(first_wide * exterior[6], interior)
    local_gram = pair_gram(columns, second)
    summed = lax.psum(local_gram, ("lon", "lat"))
    cell_total = lax.axis_size("lon") * lon_count * lax.axis_size("lat") * lat_count
    return (second[:sketch_count], summed / cell_total)


def solution(mesh):
    in_specs = (
        P(None, "lon", "lat"),
        P(None, "lon", "lat"),
        P("lon", "lat"),
        P("lon", "lat"),
        P("lon", "lat"),
        P("lon", "lat"),
        P("lon", "lat"),
    )
    out_specs = (P(None, "lon", "lat"), P())
    return jax.shard_map(local, mesh=mesh, in_specs=in_specs, out_specs=out_specs, check_vma=False)
```

profile of v0, /device:TPU:1, one launch (start us, length us, event | category | flops | bytes accessed | tf_op | source)
XLA Modules:
  0.0 201.9 jit_solution(6590594522301561050)
XLA Ops:
  0.6 0.7 bitcast_dynamic-update-slice_fusion.4
  1.4 0.7 bitcast_dynamic-update-slice_fusion.3
  2.1 0.7 bitcast_dynamic-update-slice_fusion.2
  2.8 0.7 bitcast_dynamic-update-slice_fusion.1
  3.5 0.7 bitcast_dynamic-update-slice_fusion
  4.2 16.8 %collective-permute-start = (f32[5,2,256]{2,1,0:T(2,128)S(1)}, f32[5,2,256]{2,1,0:T(2,128)S(1)}, u32[]{:S(2)}, u32[]{:S(2)}) collective-permute-start(f32[5,2,256]{2,1,0:T(2,128)S(1)} %get-tuple-element.16), channel_id=1, source_target_pairs={{0,8},{8,16},{16,24},{24,32},{32,40},{40,48},{48,56},{56,64},{64,7... | collective-permute-start | bytes 30728 | tf_op jit(solution)/shard_map/ppermute | solution.py:15
  21.1 1.9 collective-permute-start.1
  23.0 0.7 convert_element_type.7
  23.7 1.8 copy_multiply_fusion
  25.7 0.8 copy.13
  26.6 8.1 %collective-permute-done.1 = f32[5,2,256]{2,1,0:T(2,128)S(1)} collective-permute-done((f32[5,2,256]{2,1,0:T(2,128)S(1)}, f32[5,2,256]{2,1,0:T(2,128)S(1)}, u32[]{:S(2)}, u32[]{:S(2)}) %collective-permute-start.1) | collective-permute-done | bytes 10272 | tf_op jit(solution)/shard_map/ppermute | solution.py:17
  34.9 2.6 %collective-permute-start.2 = (f32[5,20,2]{2,1,0:T(8,128)S(1)}, f32[5,20,2]{2,1,0:T(8,128)S(1)}, u32[]{:S(2)}, u32[]{:S(2)}) collective-permute-start(f32[5,20,2]{2,1,0:T(8,128)S(1)} %get-tuple-element.14), channel_id=1, source_target_pairs={{0,1},{1,2},{2,3},{3,4},{4,5},{5,6},{6,7},{8,9},{9,10},{10,11},{11... | collective-permute-start | bytes 2408 | tf_op jit(solution)/shard_map/ppermute | solution.py:15
  37.5 1.3 collective-permute-start.3
  38.9 4.5 %collective-permute-start.4 = (f32[96,2,256]{2,0,1:T(8,128)S(1)}, f32[96,2,256]{2,0,1:T(8,128)S(1)}, u32[]{:S(2)}, u32[]{:S(2)}) collective-permute-start(f32[96,2,256]{2,0,1:T(8,128)S(1)} %get-tuple-element.8), channel_id=1, source_target_pairs={{0,8},{8,16},{16,24},{24,32},{32,40},{40,48},{48,56},{56,64},{64,7... | collective-permute-start | bytes 589832 | tf_op jit(solution)/shard_map/ppermute | solution.py:15
  43.4 1.9 collective-permute-start.5
  45.5 0.6 slice_bitcast_fusion.2
  46.3 0.8 fusion.27
  47.1 15.5 %collective-permute-done.5 = f32[96,2,256]{2,0,1:T(8,128)S(1)} collective-permute-done((f32[96,2,256]{2,0,1:T(8,128)S(1)}, f32[96,2,256]{2,0,1:T(8,128)S(1)}, u32[]{:S(2)}, u32[]{:S(2)}) %collective-permute-start.5) | collective-permute-done | bytes 196640 | tf_op jit(solution)/shard_map/ppermute | solution.py:17
  63.3 0.9 copy.15
  64.5 8.7 %collective-permute-start.6 = (f32[96,20,2]{0,2,1:T(2,128)S(1)}, f32[96,20,2]{0,2,1:T(2,128)}, u32[]{:S(2)}, u32[]{:S(2)}) collective-permute-start(f32[96,20,2]{0,2,1:T(2,128)S(1)} %copy.14), channel_id=1, source_target_pairs={{0,1},{1,2},{2,3},{3,4},{4,5},{5,6},{6,7},{8,9},{9,10},{10,11},{11... | collective-permute-start | bytes 46088 | tf_op jit(solution)/shard_map/ppermute | solution.py:15
  73.2 1.3 collective-permute-start.7
  74.5 1.5 fusion.31
  76.0 1.4 slice.182
  77.5 1.5 slice.196
  78.9 1.5 slice.208
  80.8 1.1 copy.16
  82.0 2.2 %pad_maximum_fusion = f32[96,20,260]{2,0,1:T(8,128)S(1)} fusion(f32[96,20,2]{2,0,1:T(8,128)S(1)} %copy.17, f32[96,2,256]{2,0,1:T(8,128)} %copy-done.2, f32[32,16,256]{2,0,1:T(8,128)S(1)} %fusion.24, f32[64,16,256]{2,0,1:T(8,128)S(1)} %copy_multiply_fusion, f32[96,2,256]{2,0,1:T(8,128)} %copy-done, f32[96,20,2]{2,0,1:T(8,128)S(1)} %copy.16), kind=kLoop, calls=%fused_computation | loop fusion | flops 2496000 | bytes 3993600 | tf_op jit(solution)/shard_map/concatenate | solution.py:13
  84.3 4.7 %fusion.3 = f32[96,18,258]{2,0,1:T(8,128)S(1)} fusion(f32[96,20,2]{2,0,1:T(8,128)S(1)} %copy.16, f32[96,2,256]{2,0,1:T(8,128)S(1)} %copy-done.3, f32[96,2,256]{2,0,1:T(8,128)S(1)} %copy-done.1, f32[32,16,256]{2,0,1:T(8,128)S(1)} %fusion.24, f32[64,16,256]{2,0,1:T(8,128)S(1)} %copy_multiply_fusion, f32[96,20,2]{2,0,1:T(8,128)S(1)} %copy.17, ...), kind=kLoop, calls=%fused_computation.5 | loop fusion | flops 8470656 | bytes 9260016 | tf_op jit(solution)/shard_map/mul | solution.py:103
  89.1 1.8 fusion.9
  90.9 1.4 fusion.17
  92.4 1.6 copy.20
  94.0 107.2 %psum.7 = f32[96,96]{1,0:T(8,128)S(1)} all-reduce(f32[96,96]{1,0:T(8,128)S(1)} %fusion.17), channel_id=1, replica_groups=mesh['lon'=64,'lat'=8] {'lon','lat'}, use_global_device_ids=true, to_apply=%region_0.0 | all-reduce | flops 9216 | bytes 73728 | tf_op jit(solution)/shard_map/psum | solution.py:105
  (62 shorter events, 2.8 us)
Async XLA Ops:
  4.2 22.4 %collective-permute-start = (f32[5,2,256]{2,1,0:T(2,128)S(1)}, f32[5,2,256]{2,1,0:T(2,128)S(1)}, u32[]{:S(2)}, u32[]{:S(2)}) collective-permute-start(f32[5,2,256]{2,1,0:T(2,128)S(1)} %get-tuple-element.16), channel_id=1, source_target_pairs={{0,8},{8,16},{16,24},{24,32},{32,40},{40,48},{48,56},{56,64},{64,7... | collective-permute-start | bytes 30728 | tf_op jit(solution)/shard_map/ppermute | solution.py:15
  21.1 13.7 %collective-permute-start.1 = (f32[5,2,256]{2,1,0:T(2,128)S(1)}, f32[5,2,256]{2,1,0:T(2,128)S(1)}, u32[]{:S(2)}, u32[]{:S(2)}) collective-permute-start(f32[5,2,256]{2,1,0:T(2,128)S(1)} %get-tuple-element.17), channel_id=1, source_target_pairs={{8,0},{16,8},{24,16},{32,24},{40,32},{48,40},{56,48},{64,56},{72,6... | collective-permute-start | bytes 30728 | tf_op jit(solution)/shard_map/ppermute | solution.py:17
  34.9 10.4 %collective-permute-start.2 = (f32[5,20,2]{2,1,0:T(8,128)S(1)}, f32[5,20,2]{2,1,0:T(8,128)S(1)}, u32[]{:S(2)}, u32[]{:S(2)}) collective-permute-start(f32[5,20,2]{2,1,0:T(8,128)S(1)} %get-tuple-element.14), channel_id=1, source_target_pairs={{0,1},{1,2},{2,3},{3,4},{4,5},{5,6},{6,7},{8,9},{9,10},{10,11},{11... | collective-permute-start | bytes 2408 | tf_op jit(solution)/shard_map/ppermute | solution.py:15
  37.5 7.8 %collective-permute-start.3 = (f32[5,20,2]{2,1,0:T(8,128)S(1)}, f32[5,20,2]{2,1,0:T(8,128)S(1)}, u32[]{:S(2)}, u32[]{:S(2)}) collective-permute-start(f32[5,20,2]{2,1,0:T(8,128)S(1)} %get-tuple-element.15), channel_id=1, source_target_pairs={{1,0},{2,1},{3,2},{4,3},{5,4},{6,5},{7,6},{9,8},{10,9},{11,10},{12... | collective-permute-start | bytes 2408 | tf_op jit(solution)/shard_map/ppermute | solution.py:17
  38.9 8.2 %collective-permute-start.4 = (f32[96,2,256]{2,0,1:T(8,128)S(1)}, f32[96,2,256]{2,0,1:T(8,128)S(1)}, u32[]{:S(2)}, u32[]{:S(2)}) collective-permute-start(f32[96,2,256]{2,0,1:T(8,128)S(1)} %get-tuple-element.8), channel_id=1, source_target_pairs={{0,8},{8,16},{16,24},{24,32},{32,40},{40,48},{48,56},{56,64},{64,7... | collective-permute-start | bytes 589832 | tf_op jit(solution)/shard_map/ppermute | solution.py:15
  43.4 19.2 %collective-permute-start.5 = (f32[96,2,256]{2,0,1:T(8,128)S(1)}, f32[96,2,256]{2,0,1:T(8,128)S(1)}, u32[]{:S(2)}, u32[]{:S(2)}) collective-permute-start(f32[96,2,256]{2,0,1:T(8,128)S(1)} %get-tuple-element.9), channel_id=1, source_target_pairs={{8,0},{16,8},{24,16},{32,24},{40,32},{48,40},{56,48},{64,56},{72,6... | collective-permute-start | bytes 589832 | tf_op jit(solution)/shard_map/ppermute | solution.py:17
  45.5 1.5 copy-start.5
  46.2 0.9 copy-start.4
  46.2 0.9 copy-start.7
  46.3 0.8 copy-start.6
  47.1 16.0 %copy-start = (f32[96,2,256]{2,0,1:T(8,128)}, f32[96,2,256]{2,0,1:T(8,128)S(1)}, u32[]{:S(2)}) copy-start(f32[96,2,256]{2,0,1:T(8,128)S(1)} %collective-permute-done.4) | copy-start | bytes 589828
  62.6 0.7 copy-start.2
  64.5 16.3 %collective-permute-start.6 = (f32[96,20,2]{0,2,1:T(2,128)S(1)}, f32[96,20,2]{0,2,1:T(2,128)}, u32[]{:S(2)}, u32[]{:S(2)}) collective-permute-start(f32[96,20,2]{0,2,1:T(2,128)S(1)} %copy.14), channel_id=1, source_target_pairs={{0,1},{1,2},{2,3},{3,4},{4,5},{5,6},{6,7},{8,9},{9,10},{10,11},{11... | collective-permute-start | bytes 46088 | tf_op jit(solution)/shard_map/ppermute | solution.py:15
  73.2 7.2 %collective-permute-start.7 = (f32[96,20,2]{0,2,1:T(2,128)}, f32[96,20,2]{0,2,1:T(2,128)S(1)}, u32[]{:S(2)}, u32[]{:S(2)}) collective-permute-start(f32[96,20,2]{0,2,1:T(2,128)} %copy.15), channel_id=1, source_target_pairs={{1,0},{2,1},{3,2},{4,3},{5,4},{6,5},{7,6},{9,8},{10,9},{11,10},{12... | collective-permute-start | bytes 46088 | tf_op jit(solution)/shard_map/ppermute | solution.py:17
  81.9 2.3 %copy-start.1 = (f32[96,2,256]{2,0,1:T(8,128)S(1)}, f32[96,2,256]{2,0,1:T(8,128)}, u32[]{:S(2)}) copy-start(f32[96,2,256]{2,0,1:T(8,128)} %copy-done) | copy-start | bytes 589828
  81.9 2.3 %copy-start.3 = (f32[96,2,256]{2,0,1:T(8,128)S(1)}, f32[96,2,256]{2,0,1:T(8,128)}, u32[]{:S(2)}) copy-start(f32[96,2,256]{2,0,1:T(8,128)} %copy-done.2) | copy-start | bytes 589828
  81.9 2.3 %copy-start.8 = (f32[18,258]{1,0:T(8,128)S(1)}, f32[18,258]{1,0:T(8,128)}, u32[]{:S(2)}) copy-start(f32[18,258]{1,0:T(8,128)} %get-tuple-element.23) | copy-start | bytes 55732
  81.9 2.3 %copy-start.9 = (f32[18,258]{1,0:T(8,128)S(1)}, f32[18,258]{1,0:T(8,128)}, u32[]{:S(2)}) copy-start(f32[18,258]{1,0:T(8,128)} %get-tuple-element.24) | copy-start | bytes 55732
  81.9 2.3 %copy-start.10 = (f32[18,258]{1,0:T(8,128)S(1)}, f32[18,258]{1,0:T(8,128)}, u32[]{:S(2)}) copy-start(f32[18,258]{1,0:T(8,128)} %get-tuple-element.25) | copy-start | bytes 55732
  81.9 2.3 %copy-start.11 = (f32[18,258]{1,0:T(8,128)S(1)}, f32[18,258]{1,0:T(8,128)}, u32[]{:S(2)}) copy-start(f32[18,258]{1,0:T(8,128)} %get-tuple-element.26) | copy-start | bytes 55732
  81.9 2.3 %copy-start.12 = (f32[18,258]{1,0:T(8,128)S(1)}, f32[18,258]{1,0:T(8,128)}, u32[]{:S(2)}) copy-start(f32[18,258]{1,0:T(8,128)} %get-tuple-element.27) | copy-start | bytes 55732
  81.9 2.3 %copy-start.13 = (f32[18,258]{1,0:T(8,128)S(1)}, f32[18,258]{1,0:T(8,128)}, u32[]{:S(2)}) copy-start(f32[18,258]{1,0:T(8,128)} %slice.196) | copy-start | bytes 55732
  81.9 2.3 %copy-start.14 = (f32[18,258]{1,0:T(8,128)S(1)}, f32[18,258]{1,0:T(8,128)}, u32[]{:S(2)}) copy-start(f32[18,258]{1,0:T(8,128)} %slice.208) | copy-start | bytes 55732
  84.3 4.8 %copy-start.15 = (f32[16,256]{1,0:T(8,128)S(1)}, f32[16,256]{1,0:T(8,128)}, u32[]{:S(2)}) copy-start(f32[16,256]{1,0:T(8,128)} %get-tuple-element.19) | copy-start | bytes 49156
  84.3 4.8 %copy-start.16 = (f32[16,256]{1,0:T(8,128)S(1)}, f32[16,256]{1,0:T(8,128)}, u32[]{:S(2)}) copy-start(f32[16,256]{1,0:T(8,128)} %get-tuple-element.20) | copy-start | bytes 49156
  84.3 4.8 %copy-start.17 = (f32[16,256]{1,0:T(8,128)S(1)}, f32[16,256]{1,0:T(8,128)}, u32[]{:S(2)}) copy-start(f32[16,256]{1,0:T(8,128)} %get-tuple-element.21) | copy-start | bytes 49156
  84.3 4.8 %copy-start.18 = (f32[16,256]{1,0:T(8,128)S(1)}, f32[16,256]{1,0:T(8,128)}, u32[]{:S(2)}) copy-start(f32[16,256]{1,0:T(8,128)} %get-tuple-element.22) | copy-start | bytes 49156
  84.3 4.8 %copy-start.19 = (f32[16,256]{1,0:T(8,128)S(1)}, f32[16,256]{1,0:T(8,128)}, u32[]{:S(2)}) copy-start(f32[16,256]{1,0:T(8,128)} %slice.182) | copy-start | bytes 49156
where the time goes:
time: 203 us; the launch traced here: 202 us
  blocking collectives  107 us (53%)
  starting transfers between devices  39.1 us (19%)
  waiting for transfers between devices  23.7 us (12%)
  other arithmetic  15.6 us (8%)
  local copies, waits for them, and re-layouts  13.8 us (7%)
    psum x1, blocking collectives, local(): summed = lax.psum(local_gram, ('lon', 'lat'))  107 us
    ppermute x4, starting transfers between devices, padded_2(): lax.ppermute(tail, axis, [(i, (i + 1) % count) for i in range(ends)])  32.7 us
    ppermute x4, waiting for transfers between devices, padded_2(): lax.ppermute(head, axis, [((i + 1) % count, i) for i in range(ends)])  23.7 us
    ppermute x4, starting transfers between devices, padded_2(): lax.ppermute(head, axis, [((i + 1) % count, i) for i in range(ends)])  6.41 us
    unnamed x45, local copies, waits for them, and re-layouts  4.79 us
    mul x1, other arithmetic, local(): second = operate(first_wide * exterior[6], interior)  4.75 us
    slice x3, local copies, waits for them, and re-layouts, window(): array[offset + shift_lon:offset + shift_lon + span_lon, offset + shift_la...  4.35 us
  transfers between devices with their start and end apart: 8, of which 2 were waited for; matrix products, arithmetic and copies ran while one was open for 6% of the time, Pallas kernels for 0%

commit v1 on v0

v1 whole, which is shorter than its diff:
```python
import jax
import jax.numpy as jnp
from jax import lax
from jax.experimental import pallas as pl
from jax.experimental.pallas import tpu as pltpu
from jax.sharding import PartitionSpec as P

MESH = pl.DeviceIdType.MESH
SK = 64
NP = 32
NC = SK + NP
I = 16
J = 256
EX = SK
MSG = SK + 8
SG = MSG
ROWS = MSG + NP
PLANE = 32
NZ = 16
PIECE = NC // PLANE
CELLS = 2097152.0


def device_at(x, y, z, c):
    return (((x * 4 + y) * 2 + z // 8) * 2 + c, z % 8)


def lane_iota(rows):
    return lax.broadcasted_iota(jnp.int32, (rows, 128), 1)


def roll(v, shift):
    return pltpu.roll(v, shift, 1)


def shift_north(u, halo):
    left, right = u[:, :128], u[:, 128:]
    rl, rr = roll(left, 127), roll(right, 127)
    last = lane_iota(u.shape[0]) == 127
    return jnp.concatenate([jnp.where(last, rr, rl), jnp.where(last, halo, rr)], axis=1)


def shift_south(u, halo):
    left, right = u[:, :128], u[:, 128:]
    rl, rr = roll(left, 1), roll(right, 1)
    first = lane_iota(u.shape[0]) == 0
    return jnp.concatenate([jnp.where(first, halo, rl), jnp.where(first, rl, rr)], axis=1)


def signs(word, rows):
    bit = lax.broadcasted_iota(jnp.int32, (16, word.shape[1]), 0)
    spread = jnp.broadcast_to(word, (16, word.shape[1]))
    return (1 - 2 * jnp.bitwise_and(jnp.right_shift(spread, bit), 1)).astype(jnp.float32)


def kernel(
    sketch, words, ocean, east, north, kappa, area,
    image, gram,
    s, w_in, oc_in, co_in, cf, haloW, haloE, sgn, packN, packS, recN, recS, edge, edN, edS,
    flux, halo2W, halo2E, out, mats, acc, pieces, rs, zb, ag,
    load_sem, small_sem, lon_send, lon_recv, lat_send, lat_recv, lon2_send, lon2_recv,
    lat2_send, lat2_recv, ar_send, ar_recv, store_sem,
):
    lon, lat = lax.axis_index("lon"), lax.axis_index("lat")
    c, zh = lax.rem(lon, 2), lax.rem(lon // 2, 2)
    y, x = lax.rem(lon // 4, 4), lon // 16
    z = zh * 8 + lat
    rank = (x * 4 + y) * 2 + c
    to_east = (lax.rem(lon + 1, 64), lat)
    to_west = (lax.rem(lon + 63, 64), lat)
    to_north = (lon, lat + 1)
    to_south = (lon, lat - 1)

    plane = []
    for p in range(1, PLANE):
        q = lax.rem(rank + p, PLANE)
        plane.append((q, device_at(q // 8, lax.rem(q // 2, 4), z, lax.rem(q, 2))))
    line = [device_at(x, y, lax.rem(z + p, NZ), c) for p in range(1, NZ)]

    recN[...] = jnp.zeros((2, 16, 128), jnp.float32)
    recS[...] = jnp.zeros((2, 16, 128), jnp.float32)

    barrier = pltpu.get_barrier_semaphore()
    peers = [to_east, to_west] + line + [d for _, d in plane]
    for d in peers:
        pl.semaphore_signal(barrier, inc=1, device_id=d, device_id_type=MESH)

    def load_row(i):
        return pltpu.make_async_copy(sketch.at[:, i, :], s.at[i, pl.ds(0, SK), :], load_sem.at[i])

    small = [
        pltpu.make_async_copy(words, w_in, small_sem.at[0]),
        pltpu.make_async_copy(ocean, oc_in, small_sem.at[1]),
    ] + [
        pltpu.make_async_copy(a, co_in.at[k], small_sem.at[2 + k])
        for k, a in enumerate((east, north, kappa, area))
    ]
    order = [0, I - 1] + list(range(1, I - 1))
    for i in order[:2]:
        load_row(i).start()
    for cp in small:
        cp.start()
    for i in order[2:]:
        load_row(i).start()

    for cp in small:
        cp.wait()

    sea = oc_in[...].astype(jnp.float32)
    for i in (0, I - 1):
        for w in range(2):
            s[i, pl.ds(EX + w, 1), :] = w_in[w, i : i + 1, :].astype(jnp.float32)
        s[i, pl.ds(EX + 2, 1), :] = sea[i : i + 1]
        s[i, pl.ds(EX + 3, 1), :] = co_in[0, i : i + 1, :]
        s[i, pl.ds(EX + 4, 4), :] = jnp.zeros((4, J), jnp.float32)
    for i in order[:2]:
        load_row(i).wait()

    pl.semaphore_wait(barrier, len(peers))

    def remote(src, dst, ss, rsem, d):
        return pltpu.make_async_remote_copy(
            src_ref=src, dst_ref=dst, send_sem=ss, recv_sem=rsem, device_id=d, device_id_type=MESH
        )

    east1 = remote(s.at[I - 1, pl.ds(0, MSG), :], haloW, lon_send.at[0], lon_recv.at[0], to_east)
    west1 = remote(s.at[0, pl.ds(0, MSG), :], haloE, lon_send.at[1], lon_recv.at[1], to_west)
    east1.start()
    west1.start()

    def both_lats(turn):
        ss, rsem = ((lat_send, lat_recv), (lat2_send, lat2_recv))[turn]
        up = remote(packN, recS.at[turn], ss.at[0], rsem.at[0], to_north)
        down = remote(packS, recN.at[turn], ss.at[1], rsem.at[1], to_south)
        return up, down

    def start_lats(turn):
        up, down = both_lats(turn)
        pl.when(lat < 7)(up.start)
        pl.when(lat > 0)(down.start)

    def wait_lats(turn):
        up, down = both_lats(turn)

        @pl.when(lat < 7)
        def _():
            up.wait_send()
            down.wait_recv()

        @pl.when(lat > 0)
        def _():
            down.wait_send()
            up.wait_recv()

    def pack_edges(rows_of):
        edge[...] = jnp.zeros((2, SK, 128), jnp.float32)

        def step(i, carry):
            mine = lane_iota(8) == i
            for g in range(SK // 8):
                rows = pl.ds(8 * g, 8)
                v = rows_of(i, rows)
                edge[0, rows, :] = jnp.where(mine, roll(v[:, 128:], i + 1), edge[0, rows, :])
                edge[1, rows, :] = jnp.where(mine, roll(v[:, :128], i), edge[1, rows, :])
            return carry

        lax.fori_loop(0, I, step, 0)
        for side, pack in enumerate((packN, packS)):
            total = edge[side, 0:8, :]
            for g in range(1, SK // 8):
                total = total + roll(edge[side, 8 * g : 8 * g + 8, :], 16 * g)
            pack[0:8, :] = total

    for i in order[2:]:
        load_row(i).wait()

    w0f, w1f = w_in[0].astype(jnp.float32), w_in[1].astype(jnp.float32)
    north_c = co_in[1]
    sides = [a[:, h * 128 : h * 128 + 128] for h in (1, 0) for a in (w0f, w1f, sea, north_c)]
    turned = jnp.transpose(jnp.concatenate(sides, axis=0))
    packN[8:16, :] = jnp.broadcast_to(turned[127:128, :], (8, 128))
    packS[8:16, :] = jnp.broadcast_to(roll(turned[0:1, :], 64), (8, 128))
    pack_edges(lambda i, rows: s[i, rows, :])
    start_lats(0)

    def own_signs(i, carry):
        for w in range(2):
            s[i, pl.ds(SG + 16 * w, 16), :] = signs(w_in[w, pl.ds(i, 1), :], 16)
        return carry

    lax.fori_loop(0, I, own_signs, 0)
    mats[...] = jnp.zeros(mats.shape, jnp.bfloat16)
    acc[...] = jnp.zeros(acc.shape, jnp.float32)

    wait_lats(0)

    def column_of(rec):
        square = jnp.transpose(jnp.broadcast_to(rec[0, 8:9, :], (128, 128)))
        return square[32:48, :], square[48:64, :]

    sea_n, _ = column_of(recN)
    sea_s, north_s = column_of(recS)
    w_n = north_c * sea * shift_north(sea, sea_n)
    w_s = shift_south(w_n, north_s * sea_s * sea[:, :128])
    cf[3] = w_n
    cf[4] = w_s
    cf[5] = co_in[3]
    cf[6] = jnp.sqrt(co_in[3])
    inner_e = co_in[0, 0 : I - 1, :] * sea[0 : I - 1] * sea[1:I]
    cf[1, 0 : I - 1, :] = inner_e
    cf[2, 1:I, :] = inner_e
    kap = co_in[2]
    mid = slice(1, I - 1)
    cf[0, mid, :] = sea[mid] * (
        kap[mid] + cf[1, mid, :] + cf[2, mid, :] + w_n[mid] + w_s[mid]
    )

    def spread(turn, rec, ed):
        for g in range(SK // 8):
            v = rec[turn, 0:8, :]
            ed[8 * g : 8 * g + 8, :] = v if g == 0 else roll(v, 128 - 16 * g)

    def spread_signs(rec, ed):
        ints = rec[0, 8:9, :].astype(jnp.int32)
        for w in range(2):
            v = signs(ints, 16)
            ed[SK + 16 * w : SK + 16 * w + 16, :] = v if w == 0 else roll(v, 128 - 16)

    for rec, ed in ((recN, edN), (recS, edS)):
        spread(0, rec, ed)
        spread_signs(rec, ed)

    def weights(i):
        return [cf[k, pl.ds(i, 1), :] for k in range(7)]

    def stencil(i, wt, here, there_e, there_w, erows):
        hn = roll(edN[erows, :], 127 - i)
        hs = roll(edS[erows, :], lax.rem(128 - i, 128))
        return (
            wt[0] * here
            - wt[1] * there_e
            - wt[2] * there_w
            - wt[3] * shift_north(here, hn)
            - wt[4] * shift_south(here, hs)
        )

    def first_row(i, east_of, west_of):
        wt = weights(i)
        for g in range(NC // 16):
            at = 16 * g if g < SK // 16 else SG + 16 * g - SK
            rows = pl.ds(at, 16)
            f = stencil(
                i, wt, s[i, rows, :], east_of(g, rows), west_of(g, rows), pl.ds(16 * g, 16)
            )
            if g < SK // 16:
                flux[i, rows, :] = wt[5] * f
            t = wt[6] * f
            high = t.astype(jnp.bfloat16)
            mats[i, pl.ds(16 * g, 16), :] = high
            mats[i, pl.ds(128 + 16 * g, 16), :] = (t - high.astype(jnp.float32)).astype(
                jnp.bfloat16
            )
        m = mats[i]
        acc[...] += lax.dot_general(
            m, m, (((1,), (1,)), ((), ())), preferred_element_type=jnp.float32
        )

    def inner_first(i, carry):
        first_row(i, lambda g, rows: s[i + 1, rows, :], lambda g, rows: s[i - 1, rows, :])
        return carry

    lax.fori_loop(1, I - 1, inner_first, 0)

    east1.wait()
    west1.wait()
    sea_e, sea_w = haloE[EX + 2 : EX + 3, :], haloW[EX + 2 : EX + 3, :]
    cf[1, I - 1 : I, :] = co_in[0, I - 1 : I, :] * sea[I - 1 : I] * sea_e
    cf[2, 0:1, :] = haloW[EX + 3 : EX + 4, :] * sea_w * sea[0:1]
    for i in (0, I - 1):
        r = slice(i, i + 1)
        cf[0, r, :] = sea[r] * (kap[r] + cf[1, r, :] + cf[2, r, :] + w_n[r] + w_s[r])
    for side, halo in enumerate((haloW, haloE)):
        for w in range(2):
            sgn[side, 16 * w : 16 * w + 16, :] = signs(
                halo[EX + w : EX + w + 1, :].astype(jnp.int32), 16
            )

    def halo_of(side, halo):
        def at(g, rows):
            if g < SK // 16:
                return halo[rows, :]
            return sgn[side, 16 * g - SK : 16 * g - SK + 16, :]

        return at

    first_row(0, lambda g, rows: s[1, rows, :], halo_of(0, haloW))
    first_row(I - 1, halo_of(1, haloE), lambda g, rows: s[I - 2, rows, :])

    east2 = remote(flux.at[I - 1], halo2W, lon2_send.at[0], lon2_recv.at[0], to_east)
    west2 = remote(flux.at[0], halo2E, lon2_send.at[1], lon2_recv.at[1], to_west)

    total = (acc[0:NC, 0:128] + acc[0:NC, 128:256]) + (
        acc[128 : 128 + NC, 0:128] + acc[128 : 128 + NC, 128:256]
    )
    for q in range(PLANE):
        pieces[q] = total[PIECE * q : PIECE * q + PIECE, :]
    for q, d in plane:
        remote(pieces.at[q], rs.at[rank], ar_send.at[0], ar_recv.at[0], d).start()
    east2.start()
    west2.start()
    rs[rank] = pieces[rank]

    pack_edges(lambda i, rows: flux[i, rows, :])
    start_lats(1)

    def wait_all(ref, n, sem):
        pltpu.make_async_copy(ref.at[pl.ds(0, n)], ref.at[pl.ds(0, n)], sem).wait()

    wait_all(rs, PLANE - 1, ar_recv.at[0])
    zb[z] = jnp.sum(rs[...], axis=0)
    for d in line:
        remote(zb.at[z], zb.at[z], ar_send.at[1], ar_recv.at[1], d).start()
    wait_all(rs, PLANE - 1, ar_send.at[0])

    wait_lats(1)
    for rec, ed in ((recN, edN), (recS, edS)):
        spread(1, rec, ed)

    def second_row(i, east_of, west_of):
        wt = weights(i)
        for g in range(SK // 16):
            rows = pl.ds(16 * g, 16)
            out[i, rows, :] = stencil(i, wt, flux[i, rows, :], east_of(rows), west_of(rows), rows)

    def inner_second(i, carry):
        second_row(i, lambda rows: flux[i + 1, rows, :], lambda rows: flux[i - 1, rows, :])
        return carry

    lax.fori_loop(1, I - 1, inner_second, 0)

    def store_row(i):
        return pltpu.make_async_copy(out.at[i], image.at[:, i, :], store_sem.at[i])

    for i in range(1, I - 1):
        store_row(i).start()

    wait_all(zb, NZ - 1, ar_recv.at[1])
    wait_all(zb, NZ - 1, ar_send.at[1])
    ag[rank] = jnp.sum(zb[...], axis=0) * (1.0 / CELLS)
    for _, d in plane:
        remote(ag.at[rank], ag.at[rank], ar_send.at[2], ar_recv.at[2], d).start()

    east2.wait()
    west2.wait()
    second_row(0, lambda rows: flux[1, rows, :], lambda rows: halo2W[rows, :])
    second_row(I - 1, lambda rows: halo2E[rows, :], lambda rows: flux[I - 2, rows, :])
    for i in (0, I - 1):
        store_row(i).start()
    wait_all(ag, PLANE - 1, ar_recv.at[2])
    wait_all(ag, PLANE - 1, ar_send.at[2])
    gram[...] = ag[...]
    for i in order:
        store_row(i).wait()


def local(sketch, probe_bits, ocean, east_cond, north_cond, kappa_sq, inv_area):
    f32 = jnp.float32

    def vmem(*shape, kind=f32):
        return pltpu.VMEM(shape, kind)

    dma = pltpu.SemaphoreType.DMA
    any_space = pl.BlockSpec(memory_space=pl.ANY)
    image, gram = pl.pallas_call(
        kernel,
        out_shape=(
            jax.ShapeDtypeStruct((SK, I, J), f32),
            jax.ShapeDtypeStruct((PLANE, PIECE, 128), f32),
        ),
        in_specs=[any_space] * 7,
        out_specs=(any_space, pl.BlockSpec(memory_space=pltpu.VMEM)),
        scratch_shapes=[
            vmem(I, ROWS, J),
            vmem(2, I, J, kind=jnp.int32),
            vmem(I, J, kind=jnp.int32),
            vmem(4, I, J),
            vmem(7, I, J),
            vmem(MSG, J),
            vmem(MSG, J),
            vmem(2, NP, J),
            vmem(16, 128),
            vmem(16, 128),
            vmem(2, 16, 128),
            vmem(2, 16, 128),
            vmem(2, SK, 128),
            vmem(NC, 128),
            vmem(NC, 128),
            vmem(I, SK, J),
            vmem(SK, J),
            vmem(SK, J),
            vmem(I, SK, J),
            vmem(I, 256, J, kind=jnp.bfloat16),
            vmem(256, 256),
            vmem(PLANE, PIECE, 128),
            vmem(PLANE, PIECE, 128),
            vmem(NZ, PIECE, 128),
            vmem(PLANE, PIECE, 128),
            dma((I,)),
            dma((6,)),
            dma((2,)),
            dma((2,)),
            dma((2,)),
            dma((2,)),
            dma((2,)),
            dma((2,)),
            dma((2,)),
            dma((2,)),
            dma((3,)),
            dma((3,)),
            dma((I,)),
        ],
        compiler_params=pltpu.CompilerParams(
            collective_id=0, has_side_effects=True, vmem_limit_bytes=56 * 2**20
        ),
        name="nystrom",
    )(sketch, probe_bits, ocean, east_cond, north_cond, kappa_sq, inv_area)
    return image, gram.reshape(NC, 128)[:, :NC]


def solution(mesh):
    cells = P("lon", "lat")
    columns = P(None, "lon", "lat")
    return jax.shard_map(
        local,
        mesh=mesh,
        in_specs=(columns, columns, cells, cells, cells, cells, cells),
        out_specs=(columns, P()),
        check_vma=False,
    )
```

time: 203 us -> 53.9 us (0.27)
  blocking collectives: 107 us -> 0 us
  Pallas kernels: 0 us -> 49.3 us
  starting transfers between devices: 39.1 us -> 0 us
  waiting for transfers between devices: 23.7 us -> 0 us
  other arithmetic: 15.6 us -> 0 us
  local copies, waits for them, and re-layouts: 13.8 us -> 3.74 us
    psum x1 -> x0, blocking collectives: 107 us -> none  [local(): summed = lax.psum(local_gram, ('lon', 'lat'))]
    pallas_call x0 -> x1, Pallas kernels: none -> 49.3 us  [local(): pl.pallas_call(kernel, out_shape=(jax.ShapeDtypeStruct((SK, I, J), f32),...]
    ppermute x8 -> x0, starting transfers between devices: 39.1 us -> none  [the longest x4 32.7 us: padded_2(): lax.ppermute(tail, axis, [(i, (i + 1) % count) for i in range(ends)])]
    ppermute x8 -> x0, waiting for transfers between devices: 23.7 us -> none  [the longest x4 23.7 us: padded_2(): lax.ppermute(head, axis, [((i + 1) % count, i) for i in range(ends)])]
    mul x6 -> x0, other arithmetic: 8.61 us -> none  [the longest x1 4.75 us: local(): second = operate(first_wide * exterior[6], interior)]
    slice x9 -> x0, local copies, waits for them, and re-layouts: 6.1 us -> none  [the longest x3 4.35 us: window(): array[offset + shift_lon:offset + shift_lon + span_lon, offset + shift_la...]
    concatenate x4 -> x0, other arithmetic: 2.54 us -> none  [padded_2(): jnp.concatenate([lax.ppermute(tail, axis, [(i, (i + 1) % count) for i in...]
    unnamed x45 -> x1, local copies, waits for them, and re-layouts: 4.79 us -> 2.26 us
  transfers between devices with their start and end apart: 8 -> 0, of which waited for: 2 -> 0; matrix products, arithmetic and copies ran while one was open for 6% -> 0% of each run, Pallas kernels for 0% -> 0%
where the time goes in v1:
time: 53.9 us; the launch traced here: 53.7 us
  Pallas kernels  49.3 us (91%)
  local copies, waits for them, and re-layouts  3.74 us (7%)
  between operations  0.64 us (1%)
    pallas_call x1, Pallas kernels, local(): pl.pallas_call(kernel, out_shape=(jax.ShapeDtypeStruct((SK, I, J), f32),...  49.3 us
    unnamed x1, local copies, waits for them, and re-layouts  2.26 us
    reshape x1, local copies, waits for them, and re-layouts, local(): return (image, gram.reshape(NC, 128)[:, :NC])  1.48 us

profile of v1, /device:TPU:1, one launch (start us, length us, event | category | flops | bytes accessed | tf_op | source)
XLA Modules:
  0.0 53.7 jit_solution(12259613286120591607)
XLA Ops:
  0.6 49.3 %nystrom.1 = (f32[64,16,256]{2,1,0:T(8,128)}, f32[32,3,128]{2,1,0:T(4,128)}) custom-call(f32[64,16,256]{2,1,0:T(8,128)} %sketch.1, s32[2,16,256]{2,1,0:T(8,128)} %words.1, s32[16,256]{1,0:T(8,128)} %ocean.1, f32[16,256]{1,0:T(8,128)} %east.1, f32[16,256]{1,0:T(8,128)} %north.1, f32[16,256]{1,0:T(8,128)} %kappa.1, f32[16,256]{1,0:T(8,128)} %area.1), custom_call_target="tpu_custom_call" | custom-call | tf_op jit(solution)/shard_map/nystrom/pallas_call | solution.py:374
  49.9 1.5 %reshape.7 = f32[96,128]{1,0:T(8,128)} reshape(f32[32,3,128]{2,1,0:T(4,128)} %get-tuple-element.5) | data formatting | bytes 98304 | tf_op jit(solution)/shard_map/reshape | solution.py:427
  51.4 2.3 %copy.10 = f32[64,16,256]{2,1,0:T(8,128)} copy(f32[64,16,256]{2,1,0:T(8,128)} %get-tuple-element.8) | data formatting | bytes 2097152

commit v2 on v1

--- a/solution.py
+++ b/solution.py
@@ -19,6 +19,12 @@
 NZ = 16
 PIECE = NC // PLANE
 CELLS = 2097152.0
+CHUNKS = ((0, 40), (40, MSG - 40))
+STEPS = sorted(
+    ((dx, dy, dc) for dx in range(4) for dy in range(4) for dc in range(2) if dx or dy or dc),
+    key=lambda d: (-min(d[0], 4 - d[0]) - min(d[1], 4 - d[1]), -d[2]),
+)
+LINE = sorted(range(1, NZ), key=lambda d: -min(d, NZ - d))
 
 
 def device_at(x, y, z, c):
@@ -56,9 +62,9 @@
 def kernel(
     sketch, words, ocean, east, north, kappa, area,
     image, gram,
-    s, w_in, oc_in, co_in, cf, haloW, haloE, sgn, packN, packS, recN, recS, edge, edN, edS,
+    s, w_in, oc_in, co_in, cf, halo, via, sgn, packN, packS, recN, recS, edge, edN, edS,
     flux, halo2W, halo2E, out, mats, acc, pieces, rs, zb, ag,
-    load_sem, small_sem, lon_send, lon_recv, lat_send, lat_recv, lon2_send, lon2_recv,
+    load_sem, small_sem, far_send, via_recv, fwd_send, far_recv, near_send, near_recv, rounds, lat_send, lat_recv, lon2_send, lon2_recv,
     lat2_send, lat2_recv, ar_send, ar_recv, store_sem,
 ):
     lon, lat = lax.axis_index("lon"), lax.axis_index("lat")
@@ -71,19 +77,35 @@
     to_north = (lon, lat + 1)
     to_south = (lon, lat - 1)
 
-    plane = []
-    for p in range(1, PLANE):
-        q = lax.rem(rank + p, PLANE)
-        plane.append((q, device_at(q // 8, lax.rem(q // 2, 4), z, lax.rem(q, 2))))
-    line = [device_at(x, y, lax.rem(z + p, NZ), c) for p in range(1, NZ)]
+    far_lon, near_lon = lax.rem(lon + 63 + 2 * c, 64), lon + 1 - 2 * c
+    lat4 = lax.rem(lat + 4, 8)
+    far_row, near_row = c * (I - 1), (1 - c) * (I - 1)
+
+    def at_plane(dx, dy, dc):
+        px, py, pc = lax.rem(x + dx, 4), lax.rem(y + dy, 4), lax.rem(c + dc, 2)
+        return (px * 4 + py) * 2 + pc, device_at(px, py, z, pc)
+
+    def at_line(d):
+        return device_at(x, y, lax.rem(z + d, NZ), c)
+
+    plane = [at_plane(*d) for d in STEPS]
+    line = [at_line(d) for d in LINE]
 
     recN[...] = jnp.zeros((2, 16, 128), jnp.float32)
     recS[...] = jnp.zeros((2, 16, 128), jnp.float32)
 
+    peers = [(far_lon, lat4)]
+    peers += [at_line(d) for d in (4, NZ - 4)]
+    peers += [at_plane(*d)[1] for d in ((2, 0, 0), (0, 2, 0))]
+    peers += [at_line(d) for d in (1, NZ - 1)]
+    peers += [at_plane(*d)[1] for d in ((1, 0, 0), (3, 0, 0), (0, 1, 0), (0, 3, 0), (0, 0, 1))]
+
+    def tell(sem):
+        for d in peers:
+            pl.semaphore_signal(sem, inc=1, device_id=d, device_id_type=MESH)
+
     barrier = pltpu.get_barrier_semaphore()
-    peers = [to_east, to_west] + line + [d for _, d in plane]
-    for d in peers:
-        pl.semaphore_signal(barrier, inc=1, device_id=d, device_id_type=MESH)
+    tell(barrier)
 
     def load_row(i):
         return pltpu.make_async_copy(sketch.at[:, i, :], s.at[i, pl.ds(0, SK), :], load_sem.at[i])
@@ -116,17 +138,10 @@
     for i in order[:2]:
         load_row(i).wait()
 
-    pl.semaphore_wait(barrier, len(peers))
-
     def remote(src, dst, ss, rsem, d):
         return pltpu.make_async_remote_copy(
             src_ref=src, dst_ref=dst, send_sem=ss, recv_sem=rsem, device_id=d, device_id_type=MESH
         )
-
-    east1 = remote(s.at[I - 1, pl.ds(0, MSG), :], haloW, lon_send.at[0], lon_recv.at[0], to_east)
-    west1 = remote(s.at[0, pl.ds(0, MSG), :], haloE, lon_send.at[1], lon_recv.at[1], to_west)
-    east1.start()
-    west1.start()
 
     def both_lats(turn):
         ss, rsem = ((lat_send, lat_recv), (lat2_send, lat2_recv))[turn]
@@ -181,8 +196,6 @@
     packN[8:16, :] = jnp.broadcast_to(turned[127:128, :], (8, 128))
     packS[8:16, :] = jnp.broadcast_to(roll(turned[0:1, :], 64), (8, 128))
     pack_edges(lambda i, rows: s[i, rows, :])
-    start_lats(0)
-
     def own_signs(i, carry):
         for w in range(2):
             s[i, pl.ds(SG + 16 * w, 16), :] = signs(w_in[w, pl.ds(i, 1), :], 16)
@@ -191,6 +204,53 @@
     lax.fori_loop(0, I, own_signs, 0)
     mats[...] = jnp.zeros(mats.shape, jnp.bfloat16)
     acc[...] = jnp.zeros(acc.shape, jnp.float32)
+
+    pl.semaphore_wait(barrier, len(peers))
+
+    early = zh == 0
+
+    def part(ref, k):
+        return ref.at[pl.ds(*CHUNKS[k]), :]
+
+    def far_copy(via_slot, k, d):
+        return remote(
+            part(s.at[far_row], k), part(via.at[via_slot], k), far_send.at[k],
+            via_recv.at[via_slot, k], d,
+        )
+
+    def swap(k):
+        return far_copy(0, k, (lon, lat4))
+
+    def lift(k):
+        return far_copy(1, k, (far_lon, lat4))
+
+    def forward(via_slot, k):
+        slot, d = ((1 - c, (far_lon, lat4)), (c, (lon, lat4)))[via_slot]
+        return remote(
+            part(via.at[via_slot], k), part(halo.at[slot], k), fwd_send.at[via_slot, k],
+            far_recv.at[k], d,
+        )
+
+    near = remote(
+        s.at[near_row, pl.ds(0, MSG), :], halo.at[c], near_send, near_recv, (near_lon, lat)
+    )
+    near_in = remote(
+        s.at[near_row, pl.ds(0, MSG), :], halo.at[1 - c], near_send, near_recv, (near_lon, lat)
+    )
+
+    @pl.when(early)
+    def _():
+        for k in range(len(CHUNKS)):
+            swap(k).start()
+
+    @pl.when(zh == 1)
+    def _():
+        for k in range(len(CHUNKS)):
+            lift(k).start()
+
+    start_lats(0)
+    near.start()
+    tell(rounds.at[0])
 
     wait_lats(0)
 
@@ -269,32 +329,44 @@
         first_row(i, lambda g, rows: s[i + 1, rows, :], lambda g, rows: s[i - 1, rows, :])
         return carry
 
+    @pl.when(early)
+    def _():
+        for k in range(len(CHUNKS)):
+            for via_slot, copy in ((1, lift(k)), (0, swap(k))):
+                copy.wait_recv()
+                forward(via_slot, k).start()
+
+    pl.semaphore_wait(rounds.at[0], len(peers))
+    tell(rounds.at[1])
+
     lax.fori_loop(1, I - 1, inner_first, 0)
 
-    east1.wait()
-    west1.wait()
+    near_in.wait_recv()
+    for k in range(len(CHUNKS)):
+        remote(part(halo.at[c], k), part(halo.at[c], k), fwd_send.at[0, k], far_recv.at[k], (lon, lat4)).wait_recv()
+    haloW, haloE = halo.at[0], halo.at[1]
     sea_e, sea_w = haloE[EX + 2 : EX + 3, :], haloW[EX + 2 : EX + 3, :]
     cf[1, I - 1 : I, :] = co_in[0, I - 1 : I, :] * sea[I - 1 : I] * sea_e
     cf[2, 0:1, :] = haloW[EX + 3 : EX + 4, :] * sea_w * sea[0:1]
     for i in (0, I - 1):
         r = slice(i, i + 1)
         cf[0, r, :] = sea[r] * (kap[r] + cf[1, r, :] + cf[2, r, :] + w_n[r] + w_s[r])
-    for side, halo in enumerate((haloW, haloE)):
+    for side in range(2):
         for w in range(2):
             sgn[side, 16 * w : 16 * w + 16, :] = signs(
-                halo[EX + w : EX + w + 1, :].astype(jnp.int32), 16
+                halo[side, EX + w : EX + w + 1, :].astype(jnp.int32), 16
             )
 
-    def halo_of(side, halo):
+    def halo_of(side):
         def at(g, rows):
             if g < SK // 16:
-                return halo[rows, :]
+                return halo[side, rows, :]
             return sgn[side, 16 * g - SK : 16 * g - SK + 16, :]
 
         return at
 
-    first_row(0, lambda g, rows: s[1, rows, :], halo_of(0, haloW))
-    first_row(I - 1, halo_of(1, haloE), lambda g, rows: s[I - 2, rows, :])
+    first_row(0, lambda g, rows: s[1, rows, :], halo_of(0))
+    first_row(I - 1, halo_of(1), lambda g, rows: s[I - 2, rows, :])
 
     east2 = remote(flux.at[I - 1], halo2W, lon2_send.at[0], lon2_recv.at[0], to_east)
     west2 = remote(flux.at[0], halo2E, lon2_send.at[1], lon2_recv.at[1], to_west)
@@ -304,10 +376,9 @@
     )
     for q in range(PLANE):
         pieces[q] = total[PIECE * q : PIECE * q + PIECE, :]
+    pl.semaphore_wait(rounds.at[1], len(peers))
     for q, d in plane:
         remote(pieces.at[q], rs.at[rank], ar_send.at[0], ar_recv.at[0], d).start()
-    east2.start()
-    west2.start()
     rs[rank] = pieces[rank]
 
     pack_edges(lambda i, rows: flux[i, rows, :])
@@ -321,6 +392,8 @@
     for d in line:
         remote(zb.at[z], zb.at[z], ar_send.at[1], ar_recv.at[1], d).start()
     wait_all(rs, PLANE - 1, ar_send.at[0])
+    east2.start()
+    west2.start()
 
     wait_lats(1)
     for rec, ed in ((recN, edN), (recS, edS)):
@@ -358,9 +431,19 @@
         store_row(i).start()
     wait_all(ag, PLANE - 1, ar_recv.at[2])
     wait_all(ag, PLANE - 1, ar_send.at[2])
-    gram[...] = ag[...]
+    for q in range(PLANE):
+        gram[PIECE * q : PIECE * q + PIECE, :] = ag[q, :, 0:NC]
     for i in order:
         store_row(i).wait()
+    near.wait_send()
+    for k in range(len(CHUNKS)):
+        swap(k).wait_send()
+
+    @pl.when(early)
+    def _():
+        for k in range(len(CHUNKS)):
+            for via_slot in range(2):
+                forward(via_slot, k).wait_send()
 
 
 def local(sketch, probe_bits, ocean, east_cond, north_cond, kappa_sq, inv_area):
@@ -374,10 +457,10 @@
     image, gram = pl.pallas_call(
         kernel,
         out_shape=(
-            jax.ShapeDtypeStruct((SK, I, J), f32),
-            jax.ShapeDtypeStruct((PLANE, PIECE, 128), f32),
+            pltpu.VMEM((SK, I, J), f32),
+            pltpu.VMEM((NC, NC), f32),
         ),
-        in_specs=[any_space] * 7,
+        in_specs=[pl.BlockSpec(memory_space=pltpu.HBM)] * 7,
         out_specs=(any_space, pl.BlockSpec(memory_space=pltpu.VMEM)),
         scratch_shapes=[
             vmem(I, ROWS, J),
@@ -385,8 +468,8 @@
             vmem(I, J, kind=jnp.int32),
             vmem(4, I, J),
             vmem(7, I, J),
-            vmem(MSG, J),
-            vmem(MSG, J),
+            vmem(2, MSG, J),
+            vmem(2, MSG, J),
             vmem(2, NP, J),
             vmem(16, 128),
             vmem(16, 128),
@@ -407,8 +490,13 @@
             vmem(PLANE, PIECE, 128),
             dma((I,)),
             dma((6,)),
-            dma((2,)),
-            dma((2,)),
+            dma((len(CHUNKS),)),
+            dma((2, len(CHUNKS))),
+            dma((2, len(CHUNKS))),
+            dma((len(CHUNKS),)),
+            dma,
+            dma,
+            pltpu.SemaphoreType.REGULAR((2,)),
             dma((2,)),
             dma((2,)),
             dma((2,)),
@@ -420,11 +508,11 @@
             dma((I,)),
         ],
         compiler_params=pltpu.CompilerParams(
-            collective_id=0, has_side_effects=True, vmem_limit_bytes=56 * 2**20
+            collective_id=0, has_side_effects=True, vmem_limit_bytes=24 * 2**20
         ),
         name="nystrom",
-    )(sketch, probe_bits, ocean, east_cond, north_cond, kappa_sq, inv_area)
-    return image, gram.reshape(NC, 128)[:, :NC]
+    )(*[pltpu.with_memory_space_constraint(a, pltpu.HBM) for a in (sketch, probe_bits, ocean, east_cond, north_cond, kappa_sq, inv_area)])
+    return image, gram
 
 
 def solution(mesh):

time: 53.9 us -> 54.9 us (1.019)
  Pallas kernels: 49.3 us -> 52.5 us
  local copies, waits for them, and re-layouts: 3.74 us -> 1.59 us
    pallas_call x1, Pallas kernels: 49.3 us -> 52.5 us  [local(): pl.pallas_call(kernel, out_shape=(pltpu.VMEM((SK, I, J), f32), pltpu.VMEM...]
    reshape x1 -> x0, local copies, waits for them, and re-layouts: 1.48 us -> none  [local(): return (image, gram.reshape(NC, 128)[:, :NC])]
    unnamed x1 -> x2, local copies, waits for them, and re-layouts: 2.26 us -> 1.59 us
where the time goes in v2:
time: 54.9 us; the launch traced here: 54.7 us
  Pallas kernels  52.5 us (96%)
  local copies, waits for them, and re-layouts  1.59 us (3%)
  between operations  0.64 us (1%)
    pallas_call x1, Pallas kernels, local(): pl.pallas_call(kernel, out_shape=(pltpu.VMEM((SK, I, J), f32), pltpu.VMEM...  52.5 us
    unnamed x2, local copies, waits for them, and re-layouts  1.59 us

profile of v2, /device:TPU:1, one launch (start us, length us, event | category | flops | bytes accessed | tf_op | source)
XLA Modules:
  0.0 54.7 jit_solution(18268191823661245364)
XLA Ops:
  0.6 52.5 %nystrom.1 = (f32[64,16,256]{2,1,0:T(8,128)S(1)}, f32[96,96]{1,0:T(8,128)S(1)}) custom-call(f32[64,16,256]{2,1,0:T(8,128)} %sketch.1, s32[2,16,256]{2,1,0:T(8,128)} %words.1, s32[16,256]{1,0:T(8,128)} %ocean.1, f32[16,256]{1,0:T(8,128)} %east.1, f32[16,256]{1,0:T(8,128)} %north.1, f32[16,256]{1,0:T(8,128)} %kappa.1, f32[16,256]{1,0:T(8,128)} %area.1), custom_call_target="tpu_custom_call" | custom-call | tf_op jit(solution)/shard_map/nystrom/pallas_call | solution.py:457
  53.2 1.0 %copy.11 = f32[64,16,256]{2,1,0:T(8,128)} copy(f32[64,16,256]{2,1,0:T(8,128)S(1)} %get-tuple-element.2) | data formatting | bytes 2097152
  54.1 0.6 %copy.12 = f32[96,96]{1,0:T(8,128)} copy(f32[96,96]{1,0:T(8,128)S(1)} %get-tuple-element.3) | data formatting | bytes 73728

commit v3 on v2

v3 whole, which is shorter than its diff:
```python
import jax
import jax.numpy as jnp
from jax import lax
from jax.experimental import pallas as pl
from jax.experimental.pallas import tpu as pltpu
from jax.sharding import PartitionSpec as P

MESH = pl.DeviceIdType.MESH
SK = 64
NP = 32
NC = SK + NP
I = 16
J = 256
EX = SK
MSG = SK + 8
SG = MSG
ROWS = MSG + NP
PLANE = 32
NZ = 16
PIECE = NC // PLANE
CELLS = 2097152.0
PK = NC + SK
PKG = PK + 8
RET = SK + 8
STEPS = sorted(
    ((dx, dy, dc) for dx in range(4) for dy in range(4) for dc in range(2) if dx or dy or dc),
    key=lambda d: (-min(d[0], 4 - d[0]) - min(d[1], 4 - d[1]), -d[2]),
)
LINE = sorted(range(1, NZ), key=lambda d: -min(d, NZ - d))


def device_at(x, y, z, c):
    return (((x * 4 + y) * 2 + z // 8) * 2 + c, z % 8)


def lane_iota(rows):
    return lax.broadcasted_iota(jnp.int32, (rows, 128), 1)


def roll(v, shift):
    return pltpu.roll(v, shift, 1)


def shift_north(u, halo):
    left, right = u[:, :128], u[:, 128:]
    rl, rr = roll(left, 127), roll(right, 127)
    last = lane_iota(u.shape[0]) == 127
    return jnp.concatenate([jnp.where(last, rr, rl), jnp.where(last, halo, rr)], axis=1)


def shift_south(u, halo):
    left, right = u[:, :128], u[:, 128:]
    rl, rr = roll(left, 1), roll(right, 1)
    first = lane_iota(u.shape[0]) == 0
    return jnp.concatenate([jnp.where(first, halo, rl), jnp.where(first, rl, rr)], axis=1)


def signs(word, rows):
    bit = lax.broadcasted_iota(jnp.int32, (16, word.shape[1]), 0)
    spread = jnp.broadcast_to(word, (16, word.shape[1]))
    return (1 - 2 * jnp.bitwise_and(jnp.right_shift(spread, bit), 1)).astype(jnp.float32)


def kernel(
    sketch, words, ocean, east, north, kappa, area,
    image, gram,
    s, w_in, oc_in, co_in, cf, w_near, halo, sgn, pkg, in_pk, cor, in_cor, packN, packS, recN, recS,
    edge, edN, edS, fl, ret, out, mats, acc, pieces, rs, zb, ag,
    load_sem, small_sem, pkg_send, pkg_recv, cor_send, cor_recv, ret_send, ret_recv, near_send,
    near_recv, rounds, lat_send, lat_recv, lat2_send, lat2_recv, ar_send, ar_recv, store_sem,
):
    lon, lat = lax.axis_index("lon"), lax.axis_index("lat")
    c, zh = lax.rem(lon, 2), lax.rem(lon // 2, 2)
    y, x = lax.rem(lon // 4, 4), lon // 16
    z = zh * 8 + lat
    rank = (x * 4 + y) * 2 + c
    to_north = (lon, lat + 1)
    to_south = (lon, lat - 1)
    far_lon, near_lon = lax.rem(lon + 63 + 2 * c, 64), lon + 1 - 2 * c
    lat4 = lax.rem(lat + 4, 8)
    middle = (lax.rem(lon + 63 + c, 64), lat4)
    far_row, near_row = c * (I - 1), (1 - c) * (I - 1)
    by_far, by_near = 1 + (I - 3) * c, 1 + (I - 3) * (1 - c)

    def at_plane(dx, dy, dc):
        px, py, pc = lax.rem(x + dx, 4), lax.rem(y + dy, 4), lax.rem(c + dc, 2)
        return (px * 4 + py) * 2 + pc, device_at(px, py, z, pc)

    def at_line(d):
        return device_at(x, y, lax.rem(z + d, NZ), c)

    plane = [at_plane(*d) for d in STEPS]
    line = [at_line(d) for d in LINE]

    recN[...] = jnp.zeros((2, 16, 128), jnp.float32)
    recS[...] = jnp.zeros((2, 16, 128), jnp.float32)

    peers = [(far_lon, lat4)]
    peers += [at_line(d) for d in (4, NZ - 4)]
    peers += [at_plane(*d)[1] for d in ((2, 0, 0), (0, 2, 0))]
    peers += [at_line(d) for d in (1, NZ - 1)]
    peers += [at_plane(*d)[1] for d in ((1, 0, 0), (3, 0, 0), (0, 1, 0), (0, 3, 0), (0, 0, 1))]

    def tell(sem):
        for d in peers:
            pl.semaphore_signal(sem, inc=1, device_id=d, device_id_type=MESH)

    barrier = pltpu.get_barrier_semaphore()
    tell(barrier)

    def load_row(i):
        return pltpu.make_async_copy(sketch.at[:, i, :], s.at[i, pl.ds(0, SK), :], load_sem.at[i])

    small = [
        pltpu.make_async_copy(words, w_in, small_sem.at[0]),
        pltpu.make_async_copy(ocean, oc_in, small_sem.at[1]),
    ] + [
        pltpu.make_async_copy(a, co_in.at[k], small_sem.at[2 + k])
        for k, a in enumerate((east, north, kappa, area))
    ]
    order = [0, I - 1, 1, I - 2] + list(range(2, I - 2))
    for cp in small:
        cp.start()
    for i in order:
        load_row(i).start()
    for cp in small:
        cp.wait()

    sea = oc_in[...].astype(jnp.float32)
    for i in (0, I - 1):
        for w in range(2):
            s[i, pl.ds(EX + w, 1), :] = w_in[w, i : i + 1, :].astype(jnp.float32)
        s[i, pl.ds(EX + 2, 1), :] = sea[i : i + 1]
        s[i, pl.ds(EX + 3, 1), :] = co_in[0, i : i + 1, :]
        s[i, pl.ds(EX + 4, 1), :] = co_in[3, i : i + 1, :]
        s[i, pl.ds(EX + 5, 3), :] = jnp.zeros((3, J), jnp.float32)

    north_c, kap = co_in[1], co_in[2]
    beyond = jnp.zeros((I, 128), jnp.float32)
    w_n = north_c * sea * shift_north(sea, beyond)
    w_s = shift_south(w_n, beyond)
    inner_e = co_in[0, 0 : I - 1, :] * sea[0 : I - 1] * sea[1:I]
    cf[1, 0 : I - 1, :] = inner_e
    cf[1, I - 1 : I, :] = jnp.zeros((1, J), jnp.float32)
    cf[2, 1:I, :] = inner_e
    cf[2, 0:1, :] = jnp.zeros((1, J), jnp.float32)
    cf[3] = w_n
    cf[4] = w_s
    cf[0] = sea * (kap + cf[1] + cf[2] + w_n + w_s)
    cf[5] = co_in[3]
    cf[6] = jnp.sqrt(co_in[3])

    def own_signs(i, carry):
        for w in range(2):
            s[i, pl.ds(SG + 16 * w, 16), :] = signs(w_in[w, pl.ds(i, 1), :], 16)
        return carry

    lax.fori_loop(0, I, own_signs, 0)

    def rows_at(g):
        return pl.ds(16 * g if g < SK // 16 else SG + 16 * g - SK, 16)

    def weight(k, i):
        return cf[k, pl.ds(i, 1), :]

    for i in order[:4]:
        load_row(i).wait()
    w_inner = weight(1, (I - 2) * c)
    none = jnp.zeros((16, 128), jnp.float32)
    for g in range(NC // 16):
        here = s[far_row, rows_at(g), :]
        pkg[16 * g : 16 * g + 16, :] = (
            weight(0, far_row) * here
            - w_inner * s[by_far, rows_at(g), :]
            - weight(3, far_row) * shift_north(here, none)
            - weight(4, far_row) * shift_south(here, none)
        )
        if g < SK // 16:
            pkg[NC + 16 * g : NC + 16 * g + 16, :] = here
    pkg[PK:PKG, :] = s[far_row, pl.ds(EX, 8), :]

    def remote(src, dst, ss, rsem, d):
        return pltpu.make_async_remote_copy(
            src_ref=src, dst_ref=dst, send_sem=ss, recv_sem=rsem, device_id=d, device_id_type=MESH
        )

    def both_lats(turn):
        ss, rsem = ((lat_send, lat_recv), (lat2_send, lat2_recv))[turn]
        up = remote(packN, recS.at[turn], ss.at[0], rsem.at[0], to_north)
        down = remote(packS, recN.at[turn], ss.at[1], rsem.at[1], to_south)
        return up, down

    def start_lats(turn):
        up, down = both_lats(turn)
        pl.when(lat < 7)(up.start)
        pl.when(lat > 0)(down.start)

    def wait_lats(turn):
        up, down = both_lats(turn)

        @pl.when(lat < 7)
        def _():
            up.wait_send()
            down.wait_recv()

        @pl.when(lat > 0)
        def _():
            down.wait_send()
            up.wait_recv()

    def pack_edges(rows_of):
        edge[...] = jnp.zeros((2, SK, 128), jnp.float32)

        def step(i, carry):
            mine = lane_iota(8) == i
            for g in range(SK // 8):
                rows = pl.ds(8 * g, 8)
                v = rows_of(i, rows)
                edge[0, rows, :] = jnp.where(mine, roll(v[:, 128:], i + 1), edge[0, rows, :])
                edge[1, rows, :] = jnp.where(mine, roll(v[:, :128], i), edge[1, rows, :])
            return carry

        lax.fori_loop(0, I, step, 0)
        for side, pack in enumerate((packN, packS)):
            total = edge[side, 0:8, :]
            for g in range(1, SK // 8):
                total = total + roll(edge[side, 8 * g : 8 * g + 8, :], 16 * g)
            pack[0:8, :] = total

    for i in order[4:]:
        load_row(i).wait()

    w0f, w1f = w_in[0].astype(jnp.float32), w_in[1].astype(jnp.float32)
    sides = [a[:, h * 128 : h * 128 + 128] for h in (1, 0) for a in (w0f, w1f, sea, north_c)]
    turned = jnp.transpose(jnp.concatenate(sides, axis=0))
    packN[8:16, :] = jnp.broadcast_to(turned[127:128, :], (8, 128))
    packS[8:16, :] = jnp.broadcast_to(roll(turned[0:1, :], 64), (8, 128))
    pack_edges(lambda i, rows: s[i, rows, :])
    mats[...] = jnp.zeros(mats.shape, jnp.bfloat16)
    acc[...] = jnp.zeros(acc.shape, jnp.float32)

    pl.semaphore_wait(barrier, len(peers))

    start_lats(0)
    to_middle = remote(pkg, in_pk.at[1 - c], pkg_send, pkg_recv.at[1 - c], middle)
    to_middle.start()
    near = remote(
        s.at[near_row, pl.ds(0, MSG), :], halo, near_send.at[0], near_recv.at[0], (near_lon, lat)
    )
    near.start()
    tell(rounds.at[0])

    wait_lats(0)

    def column_of(rec):
        square = jnp.transpose(jnp.broadcast_to(rec[0, 8:9, :], (128, 128)))
        return square[32:48, :], square[48:64, :]

    def spread(turn, rec, ed):
        for g in range(SK // 8):
            v = rec[turn, 0:8, :]
            ed[8 * g : 8 * g + 8, :] = v if g == 0 else roll(v, 128 - 16 * g)

    def spread_signs(rec, ed):
        ints = rec[0, 8:9, :].astype(jnp.int32)
        for w in range(2):
            v = signs(ints, 16)
            ed[SK + 16 * w : SK + 16 * w + 16, :] = v if w == 0 else roll(v, 128 - 16)

    for rec, ed in ((recN, edN), (recS, edS)):
        spread(0, rec, ed)
        spread_signs(rec, ed)

    sea_n, _ = column_of(recN)
    sea_s, north_s = column_of(recS)
    w_n = north_c * sea * shift_north(sea, sea_n)
    w_s = shift_south(w_n, north_s * sea_s * sea[:, :128])
    cf[3] = w_n
    cf[4] = w_s
    cf[0] = sea * (kap + cf[1] + cf[2] + w_n + w_s)

    def halo_north(i, rows):
        return roll(edN[rows, :], 127 - i)

    def halo_south(i, rows):
        return roll(edS[rows, :], lax.rem(128 - i, 128))

    first, last = lane_iota(8) == 0, lane_iota(8) == 127
    total = jnp.zeros((8, 128), jnp.float32)
    wn_far, ws_far = weight(3, far_row), weight(4, far_row)
    for g in range(NC // 8):
        at = pl.ds(8 * g if g < SK // 8 else SG + 8 * g - SK, 8)
        rows = pl.ds(8 * g, 8)
        here = s[far_row, at, :]
        up = wn_far[:, 128:] * (here[:, 128:] - halo_north(far_row, rows))
        down = ws_far[:, :128] * (here[:, :128] - halo_south(far_row, rows))
        v = jnp.where(last, up, jnp.where(first, down, 0.0))
        total = total + (v if g == 0 else roll(v, 2 * g))
    cor[...] = total
    cor_to = remote(cor, in_cor.at[1 - c], cor_send, cor_recv.at[1 - c], middle)
    cor_to.start()

    pl.semaphore_wait(rounds.at[0], len(peers))
    tell(rounds.at[1])

    def stencil(i, here, across, erows):
        f = weight(0, i) * here
        for w, there in across:
            f = f - w * there
        return (
            f
            - weight(3, i) * shift_north(here, halo_north(i, erows))
            - weight(4, i) * shift_south(here, halo_south(i, erows))
        )

    def to_mats(slot, g, t):
        high = t.astype(jnp.bfloat16)
        mats[slot, pl.ds(16 * g, 16), :] = high
        mats[slot, pl.ds(128 + 16 * g, 16), :] = (t - high.astype(jnp.float32)).astype(jnp.bfloat16)

    def add_gram(slot):
        m = mats[slot]
        acc[...] += lax.dot_general(
            m, m, (((1,), (1,)), ((), ())), preferred_element_type=jnp.float32
        )

    def first_row(i, across):
        for g in range(NC // 16):
            f = stencil(i, s[i, rows_at(g), :], across(g), pl.ds(16 * g, 16))
            if g < SK // 16:
                fl[i + 1, pl.ds(16 * g, 16), :] = weight(5, i) * f
            to_mats(i, g, weight(6, i) * f)
        add_gram(i)

    def inner_first(i, carry):
        first_row(
            i,
            lambda g: (
                (weight(1, i), s[i + 1, rows_at(g), :]),
                (weight(2, i), s[i - 1, rows_at(g), :]),
            ),
        )
        return carry

    lax.fori_loop(1, I - 1, inner_first, 0)

    near.wait_recv()
    east_near = jnp.where(c == 1, halo[EX + 3 : EX + 4, :], co_in[0, I - 1 : I, :])
    w_near[...] = (
        east_near * halo[EX + 2 : EX + 3, :] * oc_in[pl.ds(near_row, 1), :].astype(jnp.float32)
    )
    cf[0, pl.ds(near_row, 1), :] += w_near[...] * oc_in[pl.ds(near_row, 1), :].astype(jnp.float32)
    for w in range(2):
        sgn[0, 16 * w : 16 * w + 16, :] = signs(halo[EX + w : EX + w + 1, :].astype(jnp.int32), 16)
    w_beside = weight(1, (I - 2) * (1 - c))

    def across_near(g):
        if g < SK // 16:
            there = halo[16 * g : 16 * g + 16, :]
        else:
            there = sgn[0, 16 * g - SK : 16 * g - SK + 16, :]
        return (w_near[...], there), (w_beside, s[by_near, rows_at(g), :])

    first_row(near_row, across_near)
    near2 = remote(
        fl.at[near_row + 1, pl.ds(0, SK), :], fl.at[c * (I + 1), pl.ds(0, SK), :],
        near_send.at[1], near_recv.at[1], (near_lon, lat),
    )
    near2.start()

    def ret_to(k):
        d = ((lon, lat4), (far_lon, lat4))[k]
        slot = (I, 0)[k]
        return remote(ret, fl.at[pl.ds(slot, 2)], ret_send.at[k], ret_recv, d)

    @pl.when(c == 1)
    def _():
        for k in range(2):
            remote(pkg, in_pk.at[k], pkg_send, pkg_recv.at[k], middle).wait_recv()
            remote(cor, in_cor.at[k], cor_send, cor_recv.at[k], middle).wait_recv()
        co = [[in_pk[k, PK + r : PK + r + 1, :] for r in range(5)] for k in range(2)]
        edge_w = co[0][3] * co[0][2] * co[1][2]
        roots = [jnp.sqrt(co[k][4]) for k in range(2)]
        ends = [lane_iota(8) == 0, lane_iota(8) == 127]
        for k in range(2):
            for w in range(2):
                sgn[k, 16 * w : 16 * w + 16, :] = signs(co[k][w].astype(jnp.int32), 16)
            ret[k, SK:RET, :] = jnp.broadcast_to(edge_w, (8, J))
        for g in range(NC // 16):
            if g < SK // 16:
                us = [in_pk[k, NC + 16 * g : NC + 16 * g + 16, :] for k in range(2)]
            else:
                us = [sgn[k, 16 * g - SK : 16 * g - SK + 16, :] for k in range(2)]
            d = edge_w * (us[0] - us[1])
            for k in range(2):
                fix = []
                for h in (2 * g, 2 * g + 1):
                    v = in_cor[k] if h == 0 else roll(in_cor[k], 128 - 2 * h)
                    fix.append(
                        jnp.concatenate([jnp.where(ends[n], v, 0.0) for n in range(2)], axis=1)
                    )
                f = in_pk[k, 16 * g : 16 * g + 16, :] + jnp.concatenate(fix, axis=0)
                f = f + d if k == 0 else f - d
                if g < SK // 16:
                    ret[k, 16 * g : 16 * g + 16, :] = co[k][4] * f
                to_mats(I - 1 + k, g, roots[k] * f)
        for k in range(2):
            ret_to(k).start()
        for k in range(2):
            add_gram(I - 1 + k)

    total = (acc[0:NC, 0:128] + acc[0:NC, 128:256]) + (
        acc[128 : 128 + NC, 0:128] + acc[128 : 128 + NC, 128:256]
    )
    for q in range(PLANE):
        pieces[q] = total[PIECE * q : PIECE * q + PIECE, :]
    pl.semaphore_wait(rounds.at[1], len(peers))
    for q, d in plane:
        remote(pieces.at[q], rs.at[rank], ar_send.at[0], ar_recv.at[0], d).start()
    rs[rank] = pieces[rank]

    def wait_all(ref, n, sem):
        pltpu.make_async_copy(ref.at[pl.ds(0, n)], ref.at[pl.ds(0, n)], sem).wait()

    wait_all(rs, PLANE - 1, ar_recv.at[0])
    zb[z] = jnp.sum(rs[...], axis=0)
    for d in line:
        remote(zb.at[z], zb.at[z], ar_send.at[1], ar_recv.at[1], d).start()
    wait_all(rs, PLANE - 1, ar_send.at[0])

    remote(ret, fl.at[pl.ds(I * c, 2)], ret_send.at[0], ret_recv, middle).wait_recv()
    near2.wait_recv()
    edge_w = fl[(I + 1) * c, SK : SK + 1, :]
    cf[1, I - 1 : I, :] = jnp.where(c == 1, edge_w, w_near[...])
    cf[2, 0:1, :] = jnp.where(c == 1, w_near[...], edge_w)
    cf[0, pl.ds(far_row, 1), :] += edge_w * oc_in[pl.ds(far_row, 1), :].astype(jnp.float32)
    pack_edges(lambda i, rows: fl[i + 1, rows, :])
    start_lats(1)
    wait_lats(1)
    for rec, ed in ((recN, edN), (recS, edS)):
        spread(1, rec, ed)

    def second_row(i, carry):
        for g in range(SK // 16):
            rows = pl.ds(16 * g, 16)
            across = (
                (weight(1, i), fl[i + 2, rows, :]),
                (weight(2, i), fl[i, rows, :]),
            )
            out[i, rows, :] = stencil(i, fl[i + 1, rows, :], across, rows)
        return carry

    lax.fori_loop(0, I, second_row, 0)

    def store_row(i):
        return pltpu.make_async_copy(out.at[i], image.at[:, i, :], store_sem.at[i])

    for i in range(I):
        store_row(i).start()

    wait_all(zb, NZ - 1, ar_recv.at[1])
    wait_all(zb, NZ - 1, ar_send.at[1])
    ag[rank] = jnp.sum(zb[...], axis=0) * (1.0 / CELLS)
    for _, d in plane:
        remote(ag.at[rank], ag.at[rank], ar_send.at[2], ar_recv.at[2], d).start()

    to_middle.wait_send()
    cor_to.wait_send()
    near.wait_send()
    near2.wait_send()

    @pl.when(c == 1)
    def _():
        for k in range(2):
            ret_to(k).wait_send()

    for i in range(I):
        store_row(i).wait()
    wait_all(ag, PLANE - 1, ar_recv.at[2])
    wait_all(ag, PLANE - 1, ar_send.at[2])
    for q in range(PLANE):
        gram[PIECE * q : PIECE * q + PIECE, :] = ag[q, :, 0:NC]


def local(sketch, probe_bits, ocean, east_cond, north_cond, kappa_sq, inv_area):
    f32 = jnp.float32

    def vmem(*shape, kind=f32):
        return pltpu.VMEM(shape, kind)

    dma = pltpu.SemaphoreType.DMA
    any_space = pl.BlockSpec(memory_space=pl.ANY)
    image, gram = pl.pallas_call(
        kernel,
        out_shape=(
            pltpu.VMEM((SK, I, J), f32),
            pltpu.VMEM((NC, NC), f32),
        ),
        in_specs=[pl.BlockSpec(memory_space=pltpu.HBM)] * 7,
        out_specs=(any_space, pl.BlockSpec(memory_space=pltpu.VMEM)),
        scratch_shapes=[
            vmem(I, ROWS, J),
            vmem(2, I, J, kind=jnp.int32),
            vmem(I, J, kind=jnp.int32),
            vmem(4, I, J),
            vmem(7, I, J),
            vmem(1, J),
            vmem(MSG, J),
            vmem(2, NP, J),
            vmem(PKG, J),
            vmem(2, PKG, J),
            vmem(8, 128),
            vmem(2, 8, 128),
            vmem(16, 128),
            vmem(16, 128),
            vmem(2, 16, 128),
            vmem(2, 16, 128),
            vmem(2, SK, 128),
            vmem(NC, 128),
            vmem(NC, 128),
            vmem(I + 2, RET, J),
            vmem(2, RET, J),
            vmem(I, SK, J),
            vmem(I + 1, 256, J, kind=jnp.bfloat16),
            vmem(256, 256),
            vmem(PLANE, PIECE, 128),
            vmem(PLANE, PIECE, 128),
            vmem(NZ, PIECE, 128),
            vmem(PLANE, PIECE, 128),
            dma((I,)),
            dma((6,)),
            dma,
            dma((2,)),
            dma,
            dma((2,)),
            dma((2,)),
            dma,
            dma((2,)),
            dma((2,)),
            pltpu.SemaphoreType.REGULAR((2,)),
            dma((2,)),
            dma((2,)),
            dma((2,)),
            dma((2,)),
            dma((3,)),
            dma((3,)),
            dma((I,)),
        ],
        compiler_params=pltpu.CompilerParams(
            collective_id=0, has_side_effects=True, vmem_limit_bytes=24 * 2**20
        ),
        name="nystrom",
    )(*[pltpu.with_memory_space_constraint(a, pltpu.HBM) for a in (sketch, probe_bits, ocean, east_cond, north_cond, kappa_sq, inv_area)])
    return image, gram


def solution(mesh):
    cells = P("lon", "lat")
    columns = P(None, "lon", "lat")
    return jax.shard_map(
        local,
        mesh=mesh,
        in_specs=(columns, columns, cells, cells, cells, cells, cells),
        out_specs=(columns, P()),
        check_vma=False,
    )
```

time: 54.9 us -> 51.8 us (0.944)
  Pallas kernels: 52.5 us -> 49.3 us
    pallas_call x1, Pallas kernels: 52.5 us -> 49.3 us  [local(): pl.pallas_call(kernel, out_shape=(pltpu.VMEM((SK, I, J), f32), pltpu.VMEM...]
where the time goes in v3:
time: 51.8 us; the launch traced here: 51.6 us
  Pallas kernels  49.3 us (95%)
  local copies, waits for them, and re-layouts  1.59 us (3%)
  between operations  0.64 us (1%)
    pallas_call x1, Pallas kernels, local(): pl.pallas_call(kernel, out_shape=(pltpu.VMEM((SK, I, J), f32), pltpu.VMEM...  49.3 us
    unnamed x2, local copies, waits for them, and re-layouts  1.59 us

profile of v3, /device:TPU:1, one launch (start us, length us, event | category | flops | bytes accessed | tf_op | source)
XLA Modules:
  0.0 51.6 jit_solution(12384433056655384215)
XLA Ops:
  0.6 49.3 %nystrom.1 = (f32[64,16,256]{2,1,0:T(8,128)S(1)}, f32[96,96]{1,0:T(8,128)S(1)}) custom-call(f32[64,16,256]{2,1,0:T(8,128)} %sketch.1, s32[2,16,256]{2,1,0:T(8,128)} %words.1, s32[16,256]{1,0:T(8,128)} %ocean.1, f32[16,256]{1,0:T(8,128)} %east.1, f32[16,256]{1,0:T(8,128)} %north.1, f32[16,256]{1,0:T(8,128)} %kappa.1, f32[16,256]{1,0:T(8,128)} %area.1), custom_call_target="tpu_custom_call" | custom-call | tf_op jit(solution)/shard_map/nystrom/pallas_call | solution.py:493
  50.0 1.0 %copy.11 = f32[64,16,256]{2,1,0:T(8,128)} copy(f32[64,16,256]{2,1,0:T(8,128)S(1)} %get-tuple-element.2) | data formatting | bytes 2097152
  50.9 0.6 %copy.12 = f32[96,96]{1,0:T(8,128)} copy(f32[96,96]{1,0:T(8,128)S(1)} %get-tuple-element.3) | data formatting | bytes 73728

commit v4 on v3

--- a/solution.py
+++ b/solution.py
@@ -65,9 +65,9 @@
     sketch, words, ocean, east, north, kappa, area,
     image, gram,
     s, w_in, oc_in, co_in, cf, w_near, halo, sgn, pkg, in_pk, cor, in_cor, packN, packS, recN, recS,
-    edge, edN, edS, fl, ret, out, mats, acc, pieces, rs, zb, ag,
+    edN, edS, fl, ret, out, mats, acc, pieces, rs, zb, ag,
     load_sem, small_sem, pkg_send, pkg_recv, cor_send, cor_recv, ret_send, ret_recv, near_send,
-    near_recv, rounds, lat_send, lat_recv, lat2_send, lat2_recv, ar_send, ar_recv, store_sem,
+    near_recv, rounds, lat_send, lat_recv, ar_send, ar_recv, store_sem,
 ):
     lon, lat = lax.axis_index("lon"), lax.axis_index("lat")
     c, zh = lax.rem(lon, 2), lax.rem(lon // 2, 2)
@@ -92,8 +92,8 @@
     plane = [at_plane(*d) for d in STEPS]
     line = [at_line(d) for d in LINE]
 
-    recN[...] = jnp.zeros((2, 16, 128), jnp.float32)
-    recS[...] = jnp.zeros((2, 16, 128), jnp.float32)
+    recN[...] = jnp.zeros((3, 16, 128), jnp.float32)
+    recS[...] = jnp.zeros((3, 16, 128), jnp.float32)
 
     peers = [(far_lon, lat4)]
     peers += [at_line(d) for d in (4, NZ - 4)]
@@ -155,7 +155,8 @@
             s[i, pl.ds(SG + 16 * w, 16), :] = signs(w_in[w, pl.ds(i, 1), :], 16)
         return carry
 
-    lax.fori_loop(0, I, own_signs, 0)
+    own_signs(far_row, 0)
+    own_signs(by_far, 0)
 
     def rows_at(g):
         return pl.ds(16 * g if g < SK // 16 else SG + 16 * g - SK, 16)
@@ -185,9 +186,15 @@
         )
 
     def both_lats(turn):
-        ss, rsem = ((lat_send, lat_recv), (lat2_send, lat2_recv))[turn]
-        up = remote(packN, recS.at[turn], ss.at[0], rsem.at[0], to_north)
-        down = remote(packS, recN.at[turn], ss.at[1], rsem.at[1], to_south)
+        rows = pl.ds(0, 8 if turn else 16)
+        up = remote(
+            packN.at[turn, rows], recS.at[turn, rows], lat_send.at[turn, 0],
+            lat_recv.at[turn, 0], to_north,
+        )
+        down = remote(
+            packS.at[turn, rows], recN.at[turn, rows], lat_send.at[turn, 1],
+            lat_recv.at[turn, 1], to_south,
+        )
         return up, down
 
     def start_lats(turn):
@@ -208,40 +215,23 @@
             down.wait_send()
             up.wait_recv()
 
-    def pack_edges(rows_of):
-        edge[...] = jnp.zeros((2, SK, 128), jnp.float32)
-
-        def step(i, carry):
-            mine = lane_iota(8) == i
-            for g in range(SK // 8):
-                rows = pl.ds(8 * g, 8)
-                v = rows_of(i, rows)
-                edge[0, rows, :] = jnp.where(mine, roll(v[:, 128:], i + 1), edge[0, rows, :])
-                edge[1, rows, :] = jnp.where(mine, roll(v[:, :128], i), edge[1, rows, :])
-            return carry
-
-        lax.fori_loop(0, I, step, 0)
+    def pack_edges(turn, rows_of, ids):
+        lanes = lane_iota(8)
+        totals = [[jnp.zeros((8, 128), jnp.float32) for _ in range(4)] for _ in range(2)]
+        for g in range(SK // 8):
+            for n, i in enumerate(ids):
+                v = rows_of(i, pl.ds(8 * g, 8))
+                for side, (u, shift) in enumerate(((v[:, 128:], 1), (v[:, :128], 0))):
+                    by = 16 * g + i + shift
+                    by = by % 128 if isinstance(i, int) else lax.rem(by, 128)
+                    at = totals[side]
+                    at[n % 4] = jnp.where(lanes == 16 * g + i, roll(u, by), at[n % 4])
         for side, pack in enumerate((packN, packS)):
-            total = edge[side, 0:8, :]
-            for g in range(1, SK // 8):
-                total = total + roll(edge[side, 8 * g : 8 * g + 8, :], 16 * g)
-            pack[0:8, :] = total
-
-    for i in order[4:]:
-        load_row(i).wait()
-
-    w0f, w1f = w_in[0].astype(jnp.float32), w_in[1].astype(jnp.float32)
-    sides = [a[:, h * 128 : h * 128 + 128] for h in (1, 0) for a in (w0f, w1f, sea, north_c)]
-    turned = jnp.transpose(jnp.concatenate(sides, axis=0))
-    packN[8:16, :] = jnp.broadcast_to(turned[127:128, :], (8, 128))
-    packS[8:16, :] = jnp.broadcast_to(roll(turned[0:1, :], 64), (8, 128))
-    pack_edges(lambda i, rows: s[i, rows, :])
-    mats[...] = jnp.zeros(mats.shape, jnp.bfloat16)
-    acc[...] = jnp.zeros(acc.shape, jnp.float32)
+            at = totals[side]
+            pack[turn, 0:8, :] = (at[0] + at[1]) + (at[2] + at[3])
 
     pl.semaphore_wait(barrier, len(peers))
 
-    start_lats(0)
     to_middle = remote(pkg, in_pk.at[1 - c], pkg_send, pkg_recv.at[1 - c], middle)
     to_middle.start()
     near = remote(
@@ -250,15 +240,30 @@
     near.start()
     tell(rounds.at[0])
 
+    for i in order[4:]:
+        load_row(i).wait()
+
+    w0f, w1f = w_in[0].astype(jnp.float32), w_in[1].astype(jnp.float32)
+    sides = [a[:, h * 128 : h * 128 + 128] for h in (1, 0) for a in (w0f, w1f, sea, north_c)]
+    turned = jnp.transpose(jnp.concatenate(sides, axis=0))
+    packN[0, 8:16, :] = jnp.broadcast_to(turned[127:128, :], (8, 128))
+    packS[0, 8:16, :] = jnp.broadcast_to(roll(turned[0:1, :], 64), (8, 128))
+    pack_edges(0, lambda i, rows: s[i, rows, :], range(I))
+    start_lats(0)
+
+    lax.fori_loop(0, I, own_signs, 0)
+    for at in (NC, 128 + NC):
+        mats[:, at : at + 32, :] = jnp.zeros((I + 1, 32, J), jnp.bfloat16)
+    acc[...] = jnp.zeros(acc.shape, jnp.float32)
+
     wait_lats(0)
 
     def column_of(rec):
         square = jnp.transpose(jnp.broadcast_to(rec[0, 8:9, :], (128, 128)))
         return square[32:48, :], square[48:64, :]
 
-    def spread(turn, rec, ed):
+    def spread(v, ed):
         for g in range(SK // 8):
-            v = rec[turn, 0:8, :]
             ed[8 * g : 8 * g + 8, :] = v if g == 0 else roll(v, 128 - 16 * g)
 
     def spread_signs(rec, ed):
@@ -268,7 +273,7 @@
             ed[SK + 16 * w : SK + 16 * w + 16, :] = v if w == 0 else roll(v, 128 - 16)
 
     for rec, ed in ((recN, edN), (recS, edS)):
-        spread(0, rec, ed)
+        spread(rec[0, 0:8, :], ed)
         spread_signs(rec, ed)
 
     sea_n, _ = column_of(recN)
@@ -422,24 +427,6 @@
     def wait_all(ref, n, sem):
         pltpu.make_async_copy(ref.at[pl.ds(0, n)], ref.at[pl.ds(0, n)], sem).wait()
 
-    wait_all(rs, PLANE - 1, ar_recv.at[0])
-    zb[z] = jnp.sum(rs[...], axis=0)
-    for d in line:
-        remote(zb.at[z], zb.at[z], ar_send.at[1], ar_recv.at[1], d).start()
-    wait_all(rs, PLANE - 1, ar_send.at[0])
-
-    remote(ret, fl.at[pl.ds(I * c, 2)], ret_send.at[0], ret_recv, middle).wait_recv()
-    near2.wait_recv()
-    edge_w = fl[(I + 1) * c, SK : SK + 1, :]
-    cf[1, I - 1 : I, :] = jnp.where(c == 1, edge_w, w_near[...])
-    cf[2, 0:1, :] = jnp.where(c == 1, w_near[...], edge_w)
-    cf[0, pl.ds(far_row, 1), :] += edge_w * oc_in[pl.ds(far_row, 1), :].astype(jnp.float32)
-    pack_edges(lambda i, rows: fl[i + 1, rows, :])
-    start_lats(1)
-    wait_lats(1)
-    for rec, ed in ((recN, edN), (recS, edS)):
-        spread(1, rec, ed)
-
     def second_row(i, carry):
         for g in range(SK // 16):
             rows = pl.ds(16 * g, 16)
@@ -450,20 +437,45 @@
             out[i, rows, :] = stencil(i, fl[i + 1, rows, :], across, rows)
         return carry
 
-    lax.fori_loop(0, I, second_row, 0)
-
     def store_row(i):
         return pltpu.make_async_copy(out.at[i], image.at[:, i, :], store_sem.at[i])
 
-    for i in range(I):
+    pack_edges(1, lambda i, rows: fl[i + 1, rows, :], list(range(1, I - 1)) + [near_row])
+    start_lats(1)
+    wait_lats(1)
+    for rec, ed in ((recN, edN), (recS, edS)):
+        spread(rec[1, 0:8, :], ed)
+    lax.fori_loop(2, I - 2, second_row, 0)
+    for i in range(2, I - 2):
         store_row(i).start()
 
+    wait_all(rs, PLANE - 1, ar_recv.at[0])
+    zb[z] = jnp.sum(rs[...], axis=0)
+    for d in line:
+        remote(zb.at[z], zb.at[z], ar_send.at[1], ar_recv.at[1], d).start()
+
+    remote(ret, fl.at[pl.ds(I * c, 2)], ret_send.at[0], ret_recv, middle).wait_recv()
+    pack_edges(2, lambda i, rows: fl[i + 1, rows, :], [far_row])
+    start_lats(2)
+    near2.wait_recv()
+    edge_w = fl[(I + 1) * c, SK : SK + 1, :]
+    cf[1, I - 1 : I, :] = jnp.where(c == 1, edge_w, w_near[...])
+    cf[2, 0:1, :] = jnp.where(c == 1, w_near[...], edge_w)
+    cf[0, pl.ds(far_row, 1), :] += edge_w * oc_in[pl.ds(far_row, 1), :].astype(jnp.float32)
+    wait_lats(2)
+    for rec, ed in ((recN, edN), (recS, edS)):
+        spread(rec[1, 0:8, :] + rec[2, 0:8, :], ed)
+    for i in (0, 1, I - 2, I - 1):
+        second_row(i, 0)
+        store_row(i).start()
+
     wait_all(zb, NZ - 1, ar_recv.at[1])
-    wait_all(zb, NZ - 1, ar_send.at[1])
     ag[rank] = jnp.sum(zb[...], axis=0) * (1.0 / CELLS)
     for _, d in plane:
         remote(ag.at[rank], ag.at[rank], ar_send.at[2], ar_recv.at[2], d).start()
 
+    wait_all(rs, PLANE - 1, ar_send.at[0])
+    wait_all(zb, NZ - 1, ar_send.at[1])
     to_middle.wait_send()
     cor_to.wait_send()
     near.wait_send()
@@ -480,6 +492,17 @@
     wait_all(ag, PLANE - 1, ar_send.at[2])
     for q in range(PLANE):
         gram[PIECE * q : PIECE * q + PIECE, :] = ag[q, :, 0:NC]
+
+
+def finish(image, gram, image_out, gram_out, sems):
+    copies = [pltpu.make_async_copy(gram, gram_out, sems.at[4])]
+    for k in range(4):
+        part = pl.ds(k * (SK // 4), SK // 4)
+        copies.append(pltpu.make_async_copy(image.at[part], image_out.at[part], sems.at[k]))
+    for copy in copies:
+        copy.start()
+    for copy in copies:
+        copy.wait()
 
 
 def local(sketch, probe_bits, ocean, east_cond, north_cond, kappa_sq, inv_area):
@@ -511,11 +534,10 @@
             vmem(2, PKG, J),
             vmem(8, 128),
             vmem(2, 8, 128),
-            vmem(16, 128),
-            vmem(16, 128),
-            vmem(2, 16, 128),
-            vmem(2, 16, 128),
-            vmem(2, SK, 128),
+            vmem(3, 16, 128),
+            vmem(3, 16, 128),
+            vmem(3, 16, 128),
+            vmem(3, 16, 128),
             vmem(NC, 128),
             vmem(NC, 128),
             vmem(I + 2, RET, J),
@@ -538,10 +560,8 @@
             dma((2,)),
             dma((2,)),
             pltpu.SemaphoreType.REGULAR((2,)),
-            dma((2,)),
-            dma((2,)),
-            dma((2,)),
-            dma((2,)),
+            dma((3, 2)),
+            dma((3, 2)),
             dma((3,)),
             dma((3,)),
             dma((I,)),
@@ -551,7 +571,17 @@
         ),
         name="nystrom",
     )(*[pltpu.with_memory_space_constraint(a, pltpu.HBM) for a in (sketch, probe_bits, ocean, east_cond, north_cond, kappa_sq, inv_area)])
-    return image, gram
+    return pl.pallas_call(
+        finish,
+        out_shape=(
+            jax.ShapeDtypeStruct((SK, I, J), f32),
+            jax.ShapeDtypeStruct((NC, NC), f32),
+        ),
+        in_specs=[pl.BlockSpec(memory_space=pltpu.VMEM)] * 2,
+        out_specs=(any_space, any_space),
+        scratch_shapes=[dma((5,))],
+        name="finish",
+    )(*[pltpu.with_memory_space_constraint(a, pltpu.VMEM) for a in (image, gram)])
 
 
 def solution(mesh):

time: 51.8 us -> 56.4 us (1.089)
  Pallas kernels: 49.3 us -> 55.6 us
  local copies, waits for them, and re-layouts: 1.59 us -> 0 us
    pallas_call x1, Pallas kernels: 49.3 us -> 54.6 us  [local(): pl.pallas_call(kernel, out_shape=(pltpu.VMEM((SK, I, J), f32), pltpu.VMEM...]
    unnamed x2 -> x0, local copies, waits for them, and re-layouts: 1.59 us -> none
    pallas_call x0 -> x1, Pallas kernels: none -> 1.02 us  [local(): pl.pallas_call(finish, out_shape=(jax.ShapeDtypeStruct((SK, I, J), f32),...]
where the time goes in v4:
time: 56.4 us; the launch traced here: 56.2 us
  Pallas kernels  55.6 us (99%)
  between operations  0.64 us (1%)
    pallas_call x1, Pallas kernels, local(): pl.pallas_call(kernel, out_shape=(pltpu.VMEM((SK, I, J), f32), pltpu.VMEM...  54.6 us

profile of v4, /device:TPU:1, one launch (start us, length us, event | category | flops | bytes accessed | tf_op | source)
XLA Modules:
  0.0 56.2 jit_solution(1497618988614161695)
XLA Ops:
  0.6 54.6 %nystrom.1 = (f32[64,16,256]{2,1,0:T(8,128)S(1)}, f32[96,96]{1,0:T(8,128)S(1)}) custom-call(f32[64,16,256]{2,1,0:T(8,128)} %sketch.1, s32[2,16,256]{2,1,0:T(8,128)} %words.1, s32[16,256]{1,0:T(8,128)} %ocean.1, f32[16,256]{1,0:T(8,128)} %east.1, f32[16,256]{1,0:T(8,128)} %north.1, f32[16,256]{1,0:T(8,128)} %kappa.1, f32[16,256]{1,0:T(8,128)} %area.1), custom_call_target="tpu_custom_call" | custom-call | tf_op jit(solution)/shard_map/nystrom/pallas_call | solution.py:516
  55.2 1.0 %finish.1 = (f32[64,16,256]{2,1,0:T(8,128)}, f32[96,96]{1,0:T(8,128)}) custom-call(f32[64,16,256]{2,1,0:T(8,128)S(1)} %get-tuple-element.4.image, f32[96,96]{1,0:T(8,128)S(1)} %get-tuple-element.5.gram), custom_call_target="tpu_custom_call" | custom-call | tf_op jit(solution)/shard_map/finish/pallas_call | solution.py:574

commit v5 on v4

--- a/solution.py
+++ b/solution.py
@@ -230,8 +230,19 @@
             at = totals[side]
             pack[turn, 0:8, :] = (at[0] + at[1]) + (at[2] + at[3])
 
+    for i in order[4:]:
+        load_row(i).wait()
+
+    w0f, w1f = w_in[0].astype(jnp.float32), w_in[1].astype(jnp.float32)
+    sides = [a[:, h * 128 : h * 128 + 128] for h in (1, 0) for a in (w0f, w1f, sea, north_c)]
+    turned = jnp.transpose(jnp.concatenate(sides, axis=0))
+    packN[0, 8:16, :] = jnp.broadcast_to(turned[127:128, :], (8, 128))
+    packS[0, 8:16, :] = jnp.broadcast_to(roll(turned[0:1, :], 64), (8, 128))
+    pack_edges(0, lambda i, rows: s[i, rows, :], range(I))
+
     pl.semaphore_wait(barrier, len(peers))
 
+    start_lats(0)
     to_middle = remote(pkg, in_pk.at[1 - c], pkg_send, pkg_recv.at[1 - c], middle)
     to_middle.start()
     near = remote(
@@ -239,17 +250,6 @@
     )
     near.start()
     tell(rounds.at[0])
-
-    for i in order[4:]:
-        load_row(i).wait()
-
-    w0f, w1f = w_in[0].astype(jnp.float32), w_in[1].astype(jnp.float32)
-    sides = [a[:, h * 128 : h * 128 + 128] for h in (1, 0) for a in (w0f, w1f, sea, north_c)]
-    turned = jnp.transpose(jnp.concatenate(sides, axis=0))
-    packN[0, 8:16, :] = jnp.broadcast_to(turned[127:128, :], (8, 128))
-    packS[0, 8:16, :] = jnp.broadcast_to(roll(turned[0:1, :], 64), (8, 128))
-    pack_edges(0, lambda i, rows: s[i, rows, :], range(I))
-    start_lats(0)
 
     lax.fori_loop(0, I, own_signs, 0)
     for at in (NC, 128 + NC):
@@ -410,8 +410,6 @@
                     ret[k, 16 * g : 16 * g + 16, :] = co[k][4] * f
                 to_mats(I - 1 + k, g, roots[k] * f)
         for k in range(2):
-            ret_to(k).start()
-        for k in range(2):
             add_gram(I - 1 + k)
 
     total = (acc[0:NC, 0:128] + acc[0:NC, 128:256]) + (
@@ -453,6 +451,16 @@
     zb[z] = jnp.sum(rs[...], axis=0)
     for d in line:
         remote(zb.at[z], zb.at[z], ar_send.at[1], ar_recv.at[1], d).start()
+
+    @pl.when(c == 1)
+    def _():
+        for k in range(2):
+            ret_to(k).start()
+
+    wait_all(zb, NZ - 1, ar_recv.at[1])
+    ag[rank] = jnp.sum(zb[...], axis=0) * (1.0 / CELLS)
+    for _, d in plane:
+        remote(ag.at[rank], ag.at[rank], ar_send.at[2], ar_recv.at[2], d).start()
 
     remote(ret, fl.at[pl.ds(I * c, 2)], ret_send.at[0], ret_recv, middle).wait_recv()
     pack_edges(2, lambda i, rows: fl[i + 1, rows, :], [far_row])
@@ -468,11 +476,6 @@
     for i in (0, 1, I - 2, I - 1):
         second_row(i, 0)
         store_row(i).start()
-
-    wait_all(zb, NZ - 1, ar_recv.at[1])
-    ag[rank] = jnp.sum(zb[...], axis=0) * (1.0 / CELLS)
-    for _, d in plane:
-        remote(ag.at[rank], ag.at[rank], ar_send.at[2], ar_recv.at[2], d).start()
 
     wait_all(rs, PLANE - 1, ar_send.at[0])
     wait_all(zb, NZ - 1, ar_send.at[1])

time: 56.4 us -> 51.3 us (0.910)
  the two profiles are of different devices: /device:TPU:1 before, /device:TPU:96 now
where the time goes in v5:
time: 51.3 us; the launch traced here: 51.1 us
  Pallas kernels  50.4 us (98%)
  between operations  0.64 us (1%)
    pallas_call x1, Pallas kernels, local(): pl.pallas_call(kernel, out_shape=(pltpu.VMEM((SK, I, J), f32), pltpu.VMEM...  49.4 us

profile of v5, /device:TPU:96, one launch (start us, length us, event | category | flops | bytes accessed | tf_op | source)
XLA Modules:
  0.0 51.1 jit_solution(7450101107442513689)
XLA Ops:
  0.6 49.4 %nystrom.1 = (f32[64,16,256]{2,1,0:T(8,128)S(1)}, f32[96,96]{1,0:T(8,128)S(1)}) custom-call(f32[64,16,256]{2,1,0:T(8,128)} %sketch.1, s32[2,16,256]{2,1,0:T(8,128)} %words.1, s32[16,256]{1,0:T(8,128)} %ocean.1, f32[16,256]{1,0:T(8,128)} %east.1, f32[16,256]{1,0:T(8,128)} %north.1, f32[16,256]{1,0:T(8,128)} %kappa.1, f32[16,256]{1,0:T(8,128)} %area.1), custom_call_target="tpu_custom_call" | custom-call | tf_op jit(solution)/shard_map/nystrom/pallas_call | solution.py:519
  50.1 1.0 %finish.1 = (f32[64,16,256]{2,1,0:T(8,128)}, f32[96,96]{1,0:T(8,128)}) custom-call(f32[64,16,256]{2,1,0:T(8,128)S(1)} %get-tuple-element.4.image, f32[96,96]{1,0:T(8,128)S(1)} %get-tuple-element.5.gram), custom_call_target="tpu_custom_call" | custom-call | tf_op jit(solution)/shard_map/finish/pallas_call | solution.py:577

commit v6 on v5

--- a/solution.py
+++ b/solution.py
@@ -462,20 +462,30 @@
     for _, d in plane:
         remote(ag.at[rank], ag.at[rank], ar_send.at[2], ar_recv.at[2], d).start()
 
+    near2.wait_recv()
+    cf[1, I - 1 : I, :] = jnp.where(c == 1, cf[1, I - 1 : I, :], w_near[...])
+    cf[2, 0:1, :] = jnp.where(c == 1, w_near[...], cf[2, 0:1, :])
+    second_row(near_row, 0)
+    second_row(by_near, 0)
+    pl.when(c == 1)(lambda: store_row(0).start())
+    pl.when(c == 0)(lambda: store_row(I - 1).start())
+
     remote(ret, fl.at[pl.ds(I * c, 2)], ret_send.at[0], ret_recv, middle).wait_recv()
     pack_edges(2, lambda i, rows: fl[i + 1, rows, :], [far_row])
     start_lats(2)
-    near2.wait_recv()
     edge_w = fl[(I + 1) * c, SK : SK + 1, :]
     cf[1, I - 1 : I, :] = jnp.where(c == 1, edge_w, w_near[...])
     cf[2, 0:1, :] = jnp.where(c == 1, w_near[...], edge_w)
     cf[0, pl.ds(far_row, 1), :] += edge_w * oc_in[pl.ds(far_row, 1), :].astype(jnp.float32)
+    second_row(by_far, 0)
+    store_row(1).start()
+    store_row(I - 2).start()
     wait_lats(2)
     for rec, ed in ((recN, edN), (recS, edS)):
         spread(rec[1, 0:8, :] + rec[2, 0:8, :], ed)
-    for i in (0, 1, I - 2, I - 1):
-        second_row(i, 0)
-        store_row(i).start()
+    second_row(far_row, 0)
+    pl.when(c == 1)(lambda: store_row(I - 1).start())
+    pl.when(c == 0)(lambda: store_row(0).start())
 
     wait_all(rs, PLANE - 1, ar_send.at[0])
     wait_all(zb, NZ - 1, ar_send.at[1])

time: 51.3 us -> 50.8 us (level)
  no operation moved by 1% of the time
where the time goes in v6:
time: 50.8 us; the launch traced here: 50.6 us
  Pallas kernels  49.9 us (98%)
  between operations  0.64 us (1%)
    pallas_call x1, Pallas kernels, local(): pl.pallas_call(kernel, out_shape=(pltpu.VMEM((SK, I, J), f32), pltpu.VMEM...  48.9 us
    pallas_call x1, Pallas kernels, local(): pl.pallas_call(finish, out_shape=(jax.ShapeDtypeStruct((SK, I, J), f32),...  1.02 us

profile of v6, /device:TPU:96, one launch (start us, length us, event | category | flops | bytes accessed | tf_op | source)
XLA Modules:
  0.0 50.6 jit_solution(9036039488331808724)
XLA Ops:
  0.6 48.9 %nystrom.1 = (f32[64,16,256]{2,1,0:T(8,128)S(1)}, f32[96,96]{1,0:T(8,128)S(1)}) custom-call(f32[64,16,256]{2,1,0:T(8,128)} %sketch.1, s32[2,16,256]{2,1,0:T(8,128)} %words.1, s32[16,256]{1,0:T(8,128)} %ocean.1, f32[16,256]{1,0:T(8,128)} %east.1, f32[16,256]{1,0:T(8,128)} %north.1, f32[16,256]{1,0:T(8,128)} %kappa.1, f32[16,256]{1,0:T(8,128)} %area.1), custom_call_target="tpu_custom_call" | custom-call | tf_op jit(solution)/shard_map/nystrom/pallas_call | solution.py:529
  49.6 1.0 %finish.1 = (f32[64,16,256]{2,1,0:T(8,128)}, f32[96,96]{1,0:T(8,128)}) custom-call(f32[64,16,256]{2,1,0:T(8,128)S(1)} %get-tuple-element.4.image, f32[96,96]{1,0:T(8,128)S(1)} %get-tuple-element.5.gram), custom_call_target="tpu_custom_call" | custom-call | tf_op jit(solution)/shard_map/finish/pallas_call | solution.py:587
